TPU v7x, 32 devices: a whole 2x2x4 slice. The times are simulated.
32 devices in a mesh: dp: 4 (over y, core), seq: 8 (over z, x).
Axes of the slice: x: 2, y: 2, z: 4, core: 2. Of those that a mesh axis runs over, the one named last changes fastest.
Arguments:
- inputs: bfloat16 [4, 16384, 768], P('dp', 'seq'), may hold values from -6 to 6
- w_in: bfloat16 [768, 3352], P('seq'), may hold values from -0.21875 to 0.21875
- w_out: bfloat16 [1536, 768], P('seq'), may hold values from -0.15625 to 0.15625
- norm_gain: float32 [768], replicated, may hold values from 0.5 to 1.5
- conv_weight: float32 [4, 1792], replicated, may hold values from -3 to 3
- conv_bias: float32 [1792], replicated, may hold values from -3 to 3
- dt_bias: float32 [24], replicated, may hold values from -6 to -1
- a_log: float32 [24], replicated, may hold values from -4 to 2
- skip: float32 [24], replicated, may hold values from 0.5 to 1.5
- gate_gain: float32 [1536], replicated, may hold values from 0.5 to 1.5
- cotangent: bfloat16 [4, 16384, 768], P('dp', 'seq'), may hold values from -6 to 6
Outputs:
- mixed: bfloat16 [4, 16384, 768], P('dp', 'seq')
- grad_inputs: float32 [4, 16384, 768], P('dp', 'seq')
- grad_w_in: float32 [768, 3352], P('seq')
- grad_w_out: float32 [1536, 768], P('seq')
- grad_norm_gain: float32 [768], replicated
- grad_conv_weight: float32 [4, 1792], replicated
- grad_conv_bias: float32 [1792], replicated
- grad_dt_bias: float32 [24], replicated
- grad_a_log: float32 [24], replicated
- grad_skip: float32 [24], replicated
- grad_gate_gain: float32 [1536], replicated
All inputs are finite; a program needn't handle non-finite values.
Results may differ from a plain program's by a relative error of at most 0.012.
The roundings to bfloat16 on the way count: a program that leaves them out, or rounds other values in their place, can miss the bound.
Values may be sent and summed in bfloat16 or wider, within the bound.
No kernel may reach another device: no remote copies, remote signals or barrier semaphores. Data moves between devices by JAX's collectives and lax.ppermute only.
A program may use at most 384 MiB of HBM per device.

v0:
```python
import jax
import jax.numpy as jnp
from jax import lax
from jax.sharding import PartitionSpec as P

HEADS = 24
HEADDIM = 64
STATE = 128
SPAN = 256
HEADS_DEV = 3


EPS = 1e-05
HIGH = lax.Precision.HIGHEST


def product(left, right):
    return jnp.dot(left, right, precision=HIGH, preferred_element_type=jnp.float32)


def rms_gain(values, gain):
    return values * lax.rsqrt(jnp.mean(values * values, axis=-1, keepdims=True) + EPS) * gain


def causal_conv(signal, taps, offset):
    width = taps.shape[0]
    padded = jnp.concatenate(
        [jnp.zeros((width - 1, signal.shape[1]), signal.dtype), signal], axis=0
    )
    total = jnp.broadcast_to(offset[None, :], signal.shape)
    for shift_at in range(width):
        total = total + taps[shift_at][None, :] * padded[shift_at : shift_at + signal.shape[0]]
    return total


def span_step(state, block):
    xs, bmat, cmat, dts, rates = block
    steps = dts * rates[None, :]
    count = steps.shape[0]
    lower = (
        lax.broadcasted_iota(jnp.int32, (count, count), 0)
        >= lax.broadcasted_iota(jnp.int32, (count, count), 1)
    ).astype(steps.dtype)
    cums = product(lower, steps)
    heads_cum = cums.T
    diff = heads_cum[:, :, None] - heads_cum[:, None, :]
    decay = jnp.exp(jnp.where(lower[None] > 0, diff, 0.0)) * lower[None]
    scores = product(cmat, bmat.T)
    weights = scores[None] * decay * dts.T[:, None, :]
    intra = jnp.einsum("hts,shp->thp", weights, xs, precision=HIGH)
    inter = jnp.einsum("tn,hpn->thp", cmat, state, precision=HIGH) * jnp.exp(cums)[:, :, None]
    tail = jnp.exp(cums[-1][None, :] - cums) * dts
    new_state = state * jnp.exp(cums[-1])[:, None, None] + jnp.einsum(
        "sh,shp,sn->hpn", tail, xs, bmat, precision=HIGH
    )
    return (new_state, intra + inter)


def scan_heads(xs, bmat, cmat, dts, rates):
    total = xs.shape[0]
    count = total // SPAN
    heads, width = (xs.shape[1], xs.shape[2])
    blocks = (
        xs.reshape(count, SPAN, heads, width),
        bmat.reshape(count, SPAN, bmat.shape[1]),
        cmat.reshape(count, SPAN, cmat.shape[1]),
        dts.reshape(count, SPAN, heads),
        jnp.broadcast_to(rates[None, :], (count, heads)),
    )
    start = jnp.zeros((heads, width, bmat.shape[1]), jnp.float32)
    final, outs = lax.scan(jax.checkpoint(span_step), start, blocks)
    return outs.reshape(total, heads, width)


def head_block(signal, raw_dt, conv_weight, conv_bias, dt_bias, a_log, skip, group):
    heads = raw_dt.shape[1]
    width = heads * HEADDIM
    inner = conv_weight.shape[1] - 2 * STATE
    start = group * width
    taps = jnp.concatenate(
        [lax.dynamic_slice_in_dim(conv_weight, start, width, 1), conv_weight[:, inner:]], axis=1
    )
    offset = jnp.concatenate(
        [lax.dynamic_slice_in_dim(conv_bias, start, width, 0), conv_bias[inner:]], axis=0
    )
    mixed_in = jax.nn.silu(causal_conv(signal, taps, offset))
    xs = mixed_in[:, :width].reshape(signal.shape[0], heads, HEADDIM)
    bmat = mixed_in[:, width : width + STATE]
    cmat = mixed_in[:, width + STATE :]
    head_start = group * heads
    dts = jax.nn.softplus(raw_dt + lax.dynamic_slice_in_dim(dt_bias, head_start, heads, 0)[None, :])
    rates = -jnp.exp(lax.dynamic_slice_in_dim(a_log, head_start, heads, 0))
    skips = lax.dynamic_slice_in_dim(skip, head_start, heads, 0)
    scanned = scan_heads(xs, bmat, cmat, dts, rates) + skips[None, :, None] * xs
    return scanned.reshape(signal.shape[0], width)


def split_groups(rows, seqs, groups):
    piece = rows.shape[0] // seqs
    width = rows.shape[1] // groups
    return (
        rows.reshape(seqs, piece, groups, width)
        .transpose(0, 2, 1, 3)
        .reshape(seqs * groups, piece, width)
    )


def join_groups(parts, seqs):
    groups = parts.shape[0] // seqs
    piece, width = (parts.shape[1], parts.shape[2])
    return (
        parts.reshape(seqs, groups, piece, width)
        .transpose(0, 2, 1, 3)
        .reshape(seqs * piece, groups * width)
    )


def gated_norm(values, gates, gain):
    return rms_gain(values * jax.nn.silu(gates), gain)


def body(
    inputs,
    w_in,
    w_out,
    norm_gain,
    conv_weight,
    conv_bias,
    dt_bias,
    a_log,
    skip,
    gate_gain,
    cotangent,
):
    seqs, piece, width_d = inputs.shape
    groups = HEADS // HEADS_DEV
    full_in, full_out = (
        lax.all_gather(w_in, "seq", axis=0, tiled=True),
        lax.all_gather(w_out, "seq", axis=0, tiled=True),
    )
    inner = full_out.shape[0]
    tokens = inputs.reshape(seqs * piece, width_d).astype(jnp.float32)
    normed, norm_pull = jax.vjp(rms_gain, tokens, norm_gain)
    normed_low = normed.astype(jnp.bfloat16)
    projected = jnp.dot(normed_low, full_in, preferred_element_type=jnp.float32).astype(
        jnp.bfloat16
    )
    gate_part = projected[:, :inner]
    shared_part = projected[:, 2 * inner : 2 * inner + 2 * STATE]
    shared_all = jnp.broadcast_to(
        shared_part.reshape(seqs, 1, piece, 2 * STATE), (seqs, groups, piece, 2 * STATE)
    ).reshape(seqs * groups, piece, 2 * STATE)
    x_recv, shared_recv, dt_recv = (
        lax.all_to_all(
            split_groups(projected[:, inner : 2 * inner], seqs, groups),
            "seq",
            split_axis=0,
            concat_axis=0,
            tiled=True,
        ),
        lax.all_to_all(shared_all, "seq", split_axis=0, concat_axis=0, tiled=True),
        lax.all_to_all(
            split_groups(projected[:, 2 * inner + 2 * STATE :], seqs, groups),
            "seq",
            split_axis=0,
            concat_axis=0,
            tiled=True,
        ),
    )
    count = x_recv.shape[0]
    width_x = x_recv.shape[2]
    length = count * piece
    signal = jnp.concatenate(
        [x_recv.reshape(length, width_x), shared_recv.reshape(length, 2 * STATE)], axis=1
    ).astype(jnp.float32)
    raw_dt = dt_recv.reshape(length, dt_recv.shape[2]).astype(jnp.float32)
    group = lax.axis_index("seq") % groups

    def heads_apply(signal_in, dt_in, taps, offset, dt_shift, log_rates, skips):
        return head_block(signal_in, dt_in, taps, offset, dt_shift, log_rates, skips, group)

    head_out, head_pull = jax.vjp(
        heads_apply, signal, raw_dt, conv_weight, conv_bias, dt_bias, a_log, skip
    )
    returned = lax.all_to_all(
        head_out.astype(jnp.bfloat16).reshape(count, piece, width_x),
        "seq",
        split_axis=0,
        concat_axis=0,
        tiled=True,
    )
    scanned = join_groups(returned, seqs).astype(jnp.float32)
    normalized, gated_pull = jax.vjp(gated_norm, scanned, gate_part.astype(jnp.float32), gate_gain)
    normalized_low = normalized.astype(jnp.bfloat16)
    branch = jnp.dot(normalized_low, full_out, preferred_element_type=jnp.float32)
    mixed = (tokens + branch).astype(jnp.bfloat16).reshape(seqs, piece, width_d)
    incoming = cotangent.reshape(seqs * piece, width_d)
    grad_out_full = lax.dot_general(
        normalized_low, incoming, (((0,), (0,)), ((), ())), preferred_element_type=jnp.float32
    )
    grad_normalized = lax.dot_general(
        incoming, full_out, (((1,), (1,)), ((), ())), preferred_element_type=jnp.float32
    )
    grad_scanned, grad_gates, grad_gate_gain = gated_pull(grad_normalized)
    grad_heads = lax.all_to_all(
        split_groups(grad_scanned.astype(jnp.bfloat16), seqs, groups),
        "seq",
        split_axis=0,
        concat_axis=0,
        tiled=True,
    )
    grad_signal, grad_dt, grad_taps, grad_offset, grad_dt_bias, grad_a_log, grad_skip = head_pull(
        grad_heads.reshape(length, width_x).astype(jnp.float32)
    )
    back_x, back_shared, back_dt = (
        lax.all_to_all(
            grad_signal[:, :width_x].reshape(count, piece, width_x),
            "seq",
            split_axis=0,
            concat_axis=0,
            tiled=True,
        ),
        lax.all_to_all(
            grad_signal[:, width_x:].reshape(count, piece, 2 * STATE),
            "seq",
            split_axis=0,
            concat_axis=0,
            tiled=True,
        ),
        lax.all_to_all(
            grad_dt.reshape(count, piece, grad_dt.shape[1]),
            "seq",
            split_axis=0,
            concat_axis=0,
            tiled=True,
        ),
    )
    grad_shared = (
        back_shared.reshape(seqs, groups, piece, 2 * STATE)
        .sum(axis=1)
        .reshape(seqs * piece, 2 * STATE)
    )
    grad_projected = jnp.concatenate(
        [grad_gates, join_groups(back_x, seqs), grad_shared, join_groups(back_dt, seqs)], axis=1
    ).astype(jnp.bfloat16)
    grad_in_full = lax.dot_general(
        normed_low, grad_projected, (((0,), (0,)), ((), ())), preferred_element_type=jnp.float32
    )
    grad_normed = lax.dot_general(
        grad_projected, full_in, (((1,), (1,)), ((), ())), preferred_element_type=jnp.float32
    )
    grad_tokens, grad_norm_gain = norm_pull(grad_normed)
    grad_inputs = (incoming.astype(jnp.float32) + grad_tokens).reshape(seqs, piece, width_d)
    rows_in, rows_out = (
        lax.psum_scatter(grad_in_full, "seq", scatter_dimension=0, tiled=True),
        lax.psum_scatter(grad_out_full, "seq", scatter_dimension=0, tiled=True),
    )
    rows_in, rows_out = lax.psum((rows_in, rows_out), "dp")
    sums = lax.psum(
        (
            grad_norm_gain,
            grad_taps,
            grad_offset,
            grad_dt_bias,
            grad_a_log,
            grad_skip,
            grad_gate_gain,
        ),
        ("dp", "seq"),
    )
    return (
        mixed,
        grad_inputs,
        rows_in,
        rows_out,
        sums[0],
        sums[1],
        sums[2],
        sums[3],
        sums[4],
        sums[5],
        sums[6],
    )


def solution(mesh):
    placed = (
        P("dp", "seq", None),
        P("seq", None),
        P("seq", None),
        P(),
        P(),
        P(),
        P(),
        P(),
        P(),
        P(),
        P("dp", "seq", None),
    )
    return jax.shard_map(
        body,
        mesh=mesh,
        in_specs=placed,
        out_specs=(
            P("dp", "seq", None),
            P("dp", "seq", None),
            P("seq", None),
            P("seq", None),
            P(),
            P(),
            P(),
            P(),
            P(),
            P(),
            P(),
        ),
        check_vma=False,
    )
```

profile of v0, /device:TPU:0, one launch (start us, length us, event | category | flops | bytes accessed | tf_op | source)
XLA Modules:
  0.0 4201.0 jit_solution(6492725393849516520)
XLA Ops:
  11.1 88.9 %all-gather.3.cloned.1.call-done = bf16[768,3352]{1,0:T(8,128)(2,1)} async-done(((bf16[96,3352]{1,0:T(8,128)(2,1)}), bf16[768,3352]{1,0:T(8,128)(2,1)}) %all-gather.3.cloned.1.call-update) | async-done | bytes 5148688 | tf_op jit(solution)/shard_map/all_gather | solution.py:138
  100.0 17.3 convolution_convert_fusion
  135.0 137.2 %all-to-all-done.1 = bf16[8,2048,192]{1,2,0:T(8,128)(2,1)} async-done(((bf16[8,2048,192]{1,2,0:T(8,128)(2,1)}), bf16[8,2048,192]{1,2,0:T(8,128)(2,1)}, u32[]{:S(2)}, u32[]{:S(2)}) %all-to-all-start.1) | async-done | bytes 6291488 | tf_op jit(solution)/shard_map/all_to_all | solution.py:154
  293.8 170.0 %all-to-all-done.2 = bf16[8,2048,256]{1,2,0:T(8,128)(2,1)} async-done(((bf16[8,2048,256]{1,2,0:T(8,128)(2,1)}), bf16[8,2048,256]{1,2,0:T(8,128)(2,1)}, u32[]{:S(2)}, u32[]{:S(2)}) %all-to-all-start.2) | async-done | bytes 8388640 | tf_op jit(solution)/shard_map/all_to_all | solution.py:161
  487.2 64.3 %fusion.104 = (f32[16384,448]{0,1:T(8,128)}, f32[16384,448]{0,1:T(8,128)}) fusion(f32[16384,448]{0,1:T(8,128)} %maximum_convert_fusion, f32[448]{0:T(512)} %bitcast.378, f32[448]{0:T(512)} %bitcast.380, f32[448]{0:T(512)S(1)} %bitcast.376, f32[448]{0:T(512)S(1)} %bitcast.374, f32[448]{0:T(512)} %pad_maximum_fusion.4), kind=kLoop, calls=%fused_computation.152 | loop fusion | flops 88080384 | bytes 88089344 | tf_op jit(solution)/shard_map/jvp(jit(silu))/mul | solution.py:86
  587.3 16.5 copy.66
  628.0 836.8 %while.41 = (s32[]{:T(128)}, f32[3,64,128]{2,1,0:T(8,128)S(1)}, f32[64,256,3,64]{1,0,3,2:T(8,128)}, f32[64,3,64,128]{3,2,1,0:T(8,128)}, f32[64,256,3]{1,2,0:T(4,...) while((s32[]{:T(128)}, f32[3,64,128]{2,1,0:T(8,128)S(1)}, ...), condition=%wide.region_2.3_spmd.clone, body=%wide.region_1.2_spmd.clone.sunk | while | flops 406530304 | bytes 3946760 | solution.py:71
  1464.8 20.1 copy.132
  1503.0 165.0 %all-to-all-done.3 = bf16[8,2048,192]{1,2,0:T(8,128)(2,1)} async-done(((bf16[8,2048,192]{1,2,0:T(8,128)(2,1)}), bf16[8,2048,192]{1,2,0:T(8,128)(2,1)}, u32[]{:S(2)}, u32[]{:S(2)}) %all-to-all-start.3) | async-done | bytes 6291488 | tf_op jit(solution)/shard_map/all_to_all | solution.py:185
  1693.1 16.9 fusion.110
  1715.2 137.2 %all-to-all-done.4 = bf16[8,2048,192]{1,2,0:T(8,128)(2,1)} async-done(((bf16[8,2048,192]{1,2,0:T(8,128)(2,1)}), bf16[8,2048,192]{1,2,0:T(8,128)(2,1)}, u32[]{:S(2)}, u32[]{:S(2)}) %all-to-all-start.4) | async-done | bytes 6291488 | tf_op jit(solution)/shard_map/all_to_all | solution.py:205
  1911.7 1250.8 %while.42 = (s32[]{:T(128)}, f32[3,64,128]{2,1,0:T(8,128)S(1)}, f32[64,256,3,64]{1,0,3,2:T(8,128)}, f32[64,256,128]{2,1,0:T(8,128)}, f32[64,256,128]{2,1,0:T(8,1...) while((s32[]{:T(128)}, f32[3,64,128]{2,1,0:T(8,128)S(1)}, ...), condition=%wide.region_14.15_spmd.clone, body=%wide.region_5.14_spmd.clone.sunk | while | flops 991023104 | bytes 10215895 | solution.py:71
  3162.6 20.2 copy.133
  3205.7 18.3 multiply_reduce_fusion.10
  3224.0 64.9 %multiply_reduce_fusion.7 = (f32[448]{0:T(512)}, f32[448]{0:T(512)}, f32[448]{0:T(512)}, f32[448]{0:T(512)}, f32[448]{0:T(512)}, /*index=5*/f32[16384,448]{0,1:T(8,128)}) fusion(f32[16384,448]{0,1:T(8,128)} %maximum_convert_fusion, bf16[16384,256]{0,1:T(8,128)(2,1)} %bitcast.339, bf16[16384,192]{0,1:T(8,128)(2,1)} %bitcast.342, ...), kind=kLoop, calls=%fused_computation.149 | loop fusion | flops 176158528 | bytes 132129536 | tf_op jit(solution)/shard_map/transpose(jvp())/reduce_sum | solution.py:32
  3288.9 46.0 %broadcast_multiply_fusion = (f32[16384,448]{0,1:T(8,128)}, f32[16384,448]{0,1:T(8,128)}, f32[16384,448]{0,1:T(8,128)}, f32[16384,448]{0,1:T(8,128)}) fusion(f32[16384,448]{0,1:T(8,128)} %get-tuple-element.645, f32[448]{0:T(512)S(1)} %bitcast.379, f32[448]{0:T(512)S(1)} %bitcast.375, f32[448]{0:T(512)S(1)} %bitcast.377, f32[448]{0:T(512)S(1)} %bitcast.381), kind=kLoop, calls=%fused_computation.167 | loop fusion | flops 29360128 | bytes 146807808 | tf_op jit(solution)/shard_map/transpose(jvp())/mul | solution.py:32
  3334.9 29.6 pad_add_fusion
  3382.8 19.0 pad_add_fusion.3
  3405.1 340.3 %all-to-all-done.6 = f32[8,2048,256]{1,2,0:T(8,128)} async-done(((f32[8,2048,256]{1,2,0:T(8,128)}), f32[8,2048,256]{1,2,0:T(8,128)}, u32[]{:S(2)}, u32[]{:S(2)}) %all-to-all-start.6) | async-done | bytes 16777248 | tf_op jit(solution)/shard_map/all_to_all | solution.py:223
  3769.3 156.0 %all-to-all-done.5 = bf16[8,2048,192]{1,2,0:T(8,128)(2,1)} async-done(((bf16[8,2048,192]{1,2,0:T(8,128)(2,1)}), bf16[8,2048,192]{1,2,0:T(8,128)(2,1)}, u32[]{:S(2)}, u32[]{:S(2)}) %all-to-all-start.5) | async-done | bytes 6291488 | tf_op jit(solution)/shard_map/all_to_all | solution.py:216
  3925.4 22.2 fusion.125
  3967.3 18.5 fusion.114
  3985.8 152.8 %reduce-scatter.3.cloned.1.call-done = f32[96,3352]{1,0:T(8,128)} async-done(((f32[768,3352]{1,0:T(8,128)}), f32[96,3352]{1,0:T(8,128)}) %reduce-scatter.3.cloned.1.call-update) | async-done | bytes 1287184 | tf_op jit(solution)/shard_map/reduce_scatter | solution.py:255
  4138.7 41.4 all-reduce.16
  (3003 shorter events, 2413.4 us)
Async XLA Ops:
  7.2 92.8 %all-gather.3.cloned.1.call-start = ((), (), s32[]{:S(2)}) async-start(), calls=%async_computation.10 | async-start | bytes 5971968 | tf_op jit(solution)/shard_map/all_gather | solution.py:138
  118.9 10.7 all-to-all-start
  129.6 142.6 %all-to-all-start.1 = ((bf16[8,2048,192]{1,2,0:T(8,128)(2,1)}), bf16[8,2048,192]{1,2,0:T(8,128)(2,1)}, u32[]{:S(2)}, u32[]{:S(2)}) async-start(bf16[8,2048,192]{1,2,0:T(8,128)(2,1)} %bitcast.358), calls=%async_computation.1 | async-start | bytes 12582912 | tf_op jit(solution)/shard_map/all_to_all | solution.py:154
  276.6 187.2 %all-to-all-start.2 = ((bf16[8,2048,256]{1,2,0:T(8,128)(2,1)}), bf16[8,2048,256]{1,2,0:T(8,128)(2,1)}, u32[]{:S(2)}, u32[]{:S(2)}) async-start(bf16[8,2048,256]{1,2,0:T(8,128)(2,1)} %reshape.343), calls=%async_computation.2 | async-start | bytes 16777216 | tf_op jit(solution)/shard_map/all_to_all | solution.py:161
  286.1 201.1 %copy-start.18 = (f32[1,448]{1,0:T(1,128)}, f32[1,448]{1,0:T(1,128)S(1)}, u32[]{:S(2)}) copy-start(f32[1,448]{1,0:T(1,128)S(1)} %get-tuple-element.678) | copy-start | bytes 5380
  286.1 201.1 %copy-start.20 = (f32[1,448]{1,0:T(1,128)}, f32[1,448]{1,0:T(1,128)S(1)}, u32[]{:S(2)}) copy-start(f32[1,448]{1,0:T(1,128)S(1)} %get-tuple-element.679) | copy-start | bytes 5380
  293.8 178.5 %slice-start = ((s8[6291456]{0:T(1024)(128)(4,1)}), s8[2097152]{0:T(1024)(128)(4,1)S(1)}, s32[]{:S(2)}) async-start(s8[6291456]{0:T(1024)(128)(4,1)} %bitcast.343), calls=%async_computation.15 | async-start | bytes 4194304
  1497.4 170.6 %all-to-all-start.3 = ((bf16[8,2048,192]{1,2,0:T(8,128)(2,1)}), bf16[8,2048,192]{1,2,0:T(8,128)(2,1)}, u32[]{:S(2)}, u32[]{:S(2)}) async-start(bf16[8,2048,192]{1,2,0:T(8,128)(2,1)} %bitcast.356), calls=%async_computation.3 | async-start | bytes 12582912 | tf_op jit(solution)/shard_map/all_to_all | solution.py:185
  1502.2 177.4 %all-gather.5.cloned.1.call-start = ((), (), s32[]{:S(2)}) async-start(), calls=%async_computation.11 | async-start | bytes 2654208 | tf_op jit(solution)/shard_map/all_gather | solution.py:139
  1502.9 176.6 %copy-start.2 = (bf16[1,2048,768]{2,1,0:T(8,128)(2,1)S(1)}, bf16[1,2048,768]{2,1,0:T(8,128)(2,1)}, u32[]{:S(2)}) copy-start(bf16[1,2048,768]{2,1,0:T(8,128)(2,1)} %param.25) | copy-start | bytes 9437188
  1502.9 176.6 %copy-start.26 = (f32[1536]{0:T(1024)S(1)}, f32[1536]{0:T(1024)}, u32[]{:S(2)}) copy-start(f32[1536]{0:T(1024)} %param.24) | copy-start | bytes 18436
  1710.0 142.4 %all-to-all-start.4 = ((bf16[8,2048,192]{1,2,0:T(8,128)(2,1)}), bf16[8,2048,192]{1,2,0:T(8,128)(2,1)}, u32[]{:S(2)}, u32[]{:S(2)}) async-start(bf16[8,2048,192]{1,2,0:T(8,128)(2,1)} %bitcast.357), calls=%async_computation.4 | async-start | bytes 12582912 | tf_op jit(solution)/shard_map/all_to_all | solution.py:205
  3184.0 192.2 %all-to-all-start.7 = ((bf16[8,2048,3]{1,2,0:T(4,128)(2,1)}), bf16[8,2048,3]{1,2,0:T(4,128)(2,1)S(1)}, u32[]{:S(2)}, u32[]{:S(2)}) async-start(bf16[8,2048,3]{1,2,0:T(4,128)(2,1)} %fusion.131), calls=%async_computation.7 | async-start | bytes 262144 | tf_op jit(solution)/shard_map/all_to_all | solution.py:230
  3376.2 369.2 %all-to-all-start.6 = ((f32[8,2048,256]{1,2,0:T(8,128)}), f32[8,2048,256]{1,2,0:T(8,128)}, u32[]{:S(2)}, u32[]{:S(2)}) async-start(f32[8,2048,256]{1,2,0:T(8,128)} %bitcast.340), calls=%async_computation.6 | async-start | bytes 33554432 | tf_op jit(solution)/shard_map/all_to_all | solution.py:223
  3401.7 348.5 %copy-start.3 = (bf16[1,2048,768]{2,1,0:T(8,128)(2,1)S(1)}, bf16[1,2048,768]{2,1,0:T(8,128)(2,1)}, u32[]{:S(2)}) copy-start(bf16[1,2048,768]{2,1,0:T(8,128)(2,1)} %param.25) | copy-start | bytes 9437188
  3401.7 348.5 %copy-start.15 = (f32[2048]{0:T(1024)S(1)}, f32[2048]{0:T(1024)}, u32[]{:S(2)}) copy-start(f32[2048]{0:T(1024)} %copy-done.14) | copy-start | bytes 24580
  3401.8 348.5 %copy-start.27 = (f32[1536]{0:T(1024)S(1)}, f32[1536]{0:T(1024)}, u32[]{:S(2)}) copy-start(f32[1536]{0:T(1024)} %param.24) | copy-start | bytes 18436
  3745.4 180.0 %all-to-all-start.5 = ((bf16[8,2048,192]{1,2,0:T(8,128)(2,1)}), bf16[8,2048,192]{1,2,0:T(8,128)(2,1)}, u32[]{:S(2)}, u32[]{:S(2)}) async-start(bf16[8,2048,192]{1,2,0:T(8,128)(2,1)} %bitcast.355), calls=%async_computation.5 | async-start | bytes 12582912 | tf_op jit(solution)/shard_map/all_to_all | solution.py:216
  3750.1 235.7 %reduce-scatter.5.cloned.1.call-start = ((), (), s32[]{:S(2)}) async-start(), calls=%async_computation.13 | async-start | bytes 5308416 | tf_op jit(solution)/shard_map/reduce_scatter | solution.py:256
  3759.9 378.7 %reduce-scatter.3.cloned.1.call-start = ((), (), s32[]{:S(2)}) async-start(), calls=%async_computation.12 | async-start | bytes 11943936 | tf_op jit(solution)/shard_map/reduce_scatter | solution.py:255
  3947.7 242.2 %all-reduce.20.cloned.1.call-start = ((), (), s32[]{:S(2)}) async-start(), calls=%async_computation.14 | async-start | bytes 3833856 | tf_op jit(solution)/shard_map/psum | solution.py:258
  3967.3 171.4 %copy-start.11 = (f32[2048]{0:T(1024)S(1)}, f32[2048]{0:T(1024)}, u32[]{:S(2)}) copy-start(f32[2048]{0:T(1024)} %copy-done.10) | copy-start | bytes 24580
  3967.3 171.4 %copy-start.29 = (f32[1536]{0:T(1024)S(1)}, f32[1536]{0:T(1024)}, u32[]{:S(2)}) copy-start(f32[1536]{0:T(1024)} %get-tuple-element.582) | copy-start | bytes 18436
  3967.3 212.9 %copy-start.34 = (f32[768]{0:T(1024)S(1)}, f32[768]{0:T(1024)}, u32[]{:S(2)}) copy-start(f32[768]{0:T(1024)} %param.18) | copy-start | bytes 9220
  (32 other events, 2119.5 us)
Sparse Core Ops, SparseCore 0:
  10.2 89.7 all-gather.2
  1505.2 140.1 all-gather.4
  3760.1 195.4 reduce-scatter.4
  3959.1 179.5 reduce-scatter.2
  4141.1 48.7 all-reduce.19
where the time goes:
time: 4240 us; the launch traced here: 4200 us
  waiting for transfers between devices  1350 us (32%)
  local copies, waits for them, and re-layouts  1340 us (32%)
  matrix products  977 us (23%)
  other arithmetic  428 us (10%)
    dynamic_update_slice x320, local copies, waits for them, and re-layouts, scan_heads(): final, outs = lax.scan(jax.checkpoint(span_step), start, blocks)  742 us
    all_to_all x1, waiting for transfers between devices, body(): lax.all_to_all(grad_signal[:, width_x:].reshape(count, piece, 2 * STATE),...  340 us
    dot_general x448, matrix products, product(): jnp.dot(left, right, precision=HIGH, preferred_element_type=jnp.float32)  298 us
    dot_general x192, matrix products, span_step(): intra = jnp.einsum('hts,shp->thp', weights, xs, precision=HIGH)  269 us
    squeeze x320, local copies, waits for them, and re-layouts, scan_heads(): final, outs = lax.scan(jax.checkpoint(span_step), start, blocks)  227 us
    all_to_all x1, waiting for transfers between devices, body(): lax.all_to_all(shared_all, 'seq', split_axis=0, concat_axis=0, tiled=True)  170 us
    dot_general x256, matrix products, span_step(): jnp.einsum('tn,hpn->thp', cmat, state, precision=HIGH)  166 us
    all_to_all x1, waiting for transfers between devices, body(): lax.all_to_all(head_out.astype(jnp.bfloat16).reshape(count, piece, width_...  165 us
  transfers between devices with their start and end apart: 13, of which 10 were waited for; matrix products, arithmetic and copies ran while one was open for 8% of the time, Pallas kernels for 0%

commit v1 on v0

v1 whole, which is shorter than its diff:
```python
import functools

import jax
import jax.numpy as jnp
from jax import lax
from jax.experimental import pallas as pl
from jax.experimental.pallas import tpu as pltpu
from jax.sharding import PartitionSpec as P

HEADS = 24
HEADDIM = 64
STATE = 128
LANES = 128
Q = 128
QUAD = 256
EPS = 1e-05
F32 = jnp.float32
BF16 = jnp.bfloat16
VMEM_LIMIT = 56 * 1024 * 1024


def dot(left, right, dims):
    return lax.dot_general(left, right, (dims, ((), ())), preferred_element_type=F32)


def nn(left, right):
    return dot(left, right, ((1,), (0,)))


def nt(left, right):
    return dot(left, right, ((1,), (1,)))


def tn(left, right):
    return dot(left, right, ((0,), (0,)))


def exact(left, right):
    return lax.dot_general(
        left, right, (((1,), (0,)), ((), ())), precision=lax.Precision.HIGHEST,
        preferred_element_type=F32,
    )


def split2(values):
    high = values.astype(BF16)
    rest = (values - high.astype(F32)).astype(BF16)
    return jnp.concatenate([high, rest], axis=1)


def sigmoid(values):
    return 0.5 + 0.5 * jnp.tanh(0.5 * values)


def softplus(values):
    return jnp.maximum(values, 0.0) + jnp.log1p(jnp.exp(-jnp.abs(values)))


def iotas(rows, cols):
    return (
        lax.broadcasted_iota(jnp.int32, (rows, cols), 0),
        lax.broadcasted_iota(jnp.int32, (rows, cols), 1),
    )


def head_matrices(inner):
    col_head = jnp.arange(inner) // HEADDIM
    expand = (jnp.arange(LANES)[:, None] == col_head[None, :]).astype(BF16)
    return jnp.concatenate([expand, expand], axis=0), expand.T


def block_pair(pair):
    low = lax.broadcasted_iota(jnp.int32, pair.shape, 1) < HEADDIM
    zero = jnp.zeros_like(pair)
    return jnp.concatenate([jnp.where(low, pair, zero), jnp.where(low, zero, pair)], axis=0)


def conv_columns(ext_ref, taps_ref, bias_ref, cols, rows):
    total = bias_ref[0:1, cols] + taps_ref[0:1, cols] * ext_ref[pl.ds(5, rows), cols]
    for k in range(1, 4):
        total = total + taps_ref[k : k + 1, cols] * ext_ref[pl.ds(5 + k, rows), cols]
    return total


def fill_ext(ext_ref, xbc_ref, prev_ref, halo_ref, first):
    rows = xbc_ref.shape[1]
    before = jnp.where(first, halo_ref[0].astype(F32), prev_ref[0].astype(F32))
    ext_ref[0:8, :] = before[8:16]
    ext_ref[pl.ds(8, rows), :] = xbc_ref[0].astype(F32)


def scan_kernel(
    xbc_ref, prev_ref, halo_ref, raw_ref, taps_ref, bias_ref, heads_ref, ex_ref,
    act_ref, y_ref, dt_ref, cum_ref, dev_ref, st_ref, fin_ref,
    ext_ref, state_ref, carry_ref,
):
    c = pl.program_id(1)
    width = xbc_ref.shape[2]
    inner = y_ref.shape[2]

    @pl.when(c == 0)
    def _():
        state_ref[...] = jnp.zeros_like(state_ref)
        carry_ref[...] = jnp.zeros_like(carry_ref)

    fill_ext(ext_ref, xbc_ref, prev_ref, halo_ref, c == 0)
    for start in range(0, width, QUAD):
        cols = slice(start, start + QUAD)
        half = 0.5 * conv_columns(ext_ref, taps_ref, bias_ref, cols, Q)
        act_ref[0, :, cols] = (half + half * jnp.tanh(half)).astype(BF16)

    dts = softplus(raw_ref[0].astype(F32) + heads_ref[0:1, :]) * heads_ref[3:4, :]
    row, col = iotas(Q, Q)
    lower = row >= col
    cum = exact(lower.astype(F32), dts * heads_ref[1:2, :])
    dev = cum + carry_ref[0:1, :]
    carry_ref[...] = jnp.broadcast_to(dev[Q - 1 : Q, :], carry_ref.shape)
    dt_ref[0] = dts
    cum_ref[0] = cum
    dev_ref[0] = dev
    cum_t = cum.T
    dt2 = split2(dts)
    ec2 = split2(jnp.exp(cum))
    tail2 = split2(jnp.exp(cum[Q - 1 : Q, :] - cum))

    bmat = act_ref[0, :, inner : inner + STATE]
    cmat = act_ref[0, :, inner + STATE : inner + 2 * STATE]
    bmat_t = bmat.astype(F32).T.astype(BF16)
    scores = jnp.where(lower, nt(cmat, bmat), 0.0)

    for quad in range(inner // QUAD):
        cols = slice(quad * QUAD, (quad + 1) * QUAD)
        ex = ex_ref[:, cols]
        xdt = act_ref[0, :, cols].astype(F32) * nn(dt2, ex)
        xdt_b = xdt.astype(BF16)
        xtail = (xdt * nn(tail2, ex)).astype(BF16)
        ece = nn(ec2, ex)
        parts = []
        for pair in range(2):
            heads = [quad * 4 + pair * 2, quad * 4 + pair * 2 + 1]
            mats = []
            for h in heads:
                diff = cum[:, h : h + 1] - cum_t[h : h + 1, :]
                mats.append((scores * jnp.exp(jnp.minimum(diff, 0.0))).astype(BF16))
            mat = jnp.concatenate(mats, axis=1)
            parts.append(nn(mat, block_pair(xdt_b[:, pair * LANES : (pair + 1) * LANES])))
        state = state_ref[:, cols]
        state_b = state.astype(BF16)
        st_ref[0, 0, :, cols] = state_b
        y_ref[0, :, cols] = jnp.concatenate(parts, axis=1) + ece * nn(cmat, state_b)
        new = state * ece[Q - 1 : Q, :] + nn(bmat_t, xtail)
        state_ref[:, cols] = new
        fin_ref[0, :, cols] = new


def scan_call(xbc, halo, raw, taps, bias, heads, ex, inner):
    seqs, length, width = xbc.shape
    chunks = length // Q
    whole = lambda s, c: (0, 0)
    row = lambda s, c: (s, c, 0)
    lanes = jax.ShapeDtypeStruct((seqs, length, LANES), F32)
    return pl.pallas_call(
        scan_kernel,
        grid=(seqs, chunks),
        in_specs=[
            pl.BlockSpec((1, Q, width), row),
            pl.BlockSpec((1, 16, width), lambda s, c: (s, jnp.maximum(c * (Q // 16) - 1, 0), 0)),
            pl.BlockSpec((1, 16, width), lambda s, c: (s, 0, 0)),
            pl.BlockSpec((1, Q, LANES), row),
            pl.BlockSpec(taps.shape, whole),
            pl.BlockSpec(bias.shape, whole),
            pl.BlockSpec(heads.shape, whole),
            pl.BlockSpec(ex.shape, whole),
        ],
        out_specs=[
            pl.BlockSpec((1, Q, width), row),
            pl.BlockSpec((1, Q, inner), row),
            pl.BlockSpec((1, Q, LANES), row),
            pl.BlockSpec((1, Q, LANES), row),
            pl.BlockSpec((1, Q, LANES), row),
            pl.BlockSpec((1, 1, STATE, inner), lambda s, c: (s, c, 0, 0)),
            pl.BlockSpec((1, STATE, inner), lambda s, c: (s, 0, 0)),
        ],
        out_shape=[
            jax.ShapeDtypeStruct((seqs, length, width), BF16),
            jax.ShapeDtypeStruct((seqs, length, inner), F32),
            lanes,
            lanes,
            lanes,
            jax.ShapeDtypeStruct((seqs, chunks, STATE, inner), BF16),
            jax.ShapeDtypeStruct((seqs, STATE, inner), F32),
        ],
        scratch_shapes=[
            pltpu.VMEM((Q + 8, width), F32),
            pltpu.VMEM((STATE, inner), F32),
            pltpu.VMEM((8, LANES), F32),
        ],
        compiler_params=pltpu.CompilerParams(vmem_limit_bytes=VMEM_LIMIT),
        name="scan_forward",
    )(xbc, xbc, halo, raw, taps, bias, heads, ex)


def gate_kernel(
    y_ref, act_ref, z_ref, dev_ref, sin_ref, u_ref, c_ref, w_ref, vec_ref, ex_ref, red_ref,
    mixed_ref, dy_ref, dz_ref, norm_ref, rows_ref, q2_ref, sums_ref, ds_ref,
):
    s, i = pl.program_id(0), pl.program_id(1)
    inner = y_ref.shape[2]

    @pl.when(jnp.logical_and(s == 0, i == 0))
    def _():
        sums_ref[...] = jnp.zeros_like(sums_ref)

    @pl.when(i == 0)
    def _():
        ds_ref[...] = jnp.zeros_like(ds_ref)

    cmat = act_ref[0, :, inner + STATE : inner + 2 * STATE]
    ec2 = split2(jnp.exp(dev_ref[0]))
    ece = nn(ec2, ex_ref[...])
    x = act_ref[0, :, :inner].astype(F32)
    y_loc = y_ref[0]
    y_in = ece * nn(cmat, sin_ref[0])
    y = (y_loc + y_in + vec_ref[1:2, :] * x).astype(BF16).astype(F32)
    z = z_ref[0].astype(F32)
    sig = sigmoid(z)
    silu = z * sig
    g = y * silu
    scale = lax.rsqrt(jnp.mean(g * g, axis=1, keepdims=True) + EPS)
    gain = vec_ref[0:1, :]
    gs = g * scale
    normalized = (gs * gain).astype(BF16)
    norm_ref[0] = normalized
    mixed_ref[0] = (u_ref[0].astype(F32) + nn(normalized, w_ref[...])).astype(BF16)
    gn = nt(c_ref[0], w_ref[...])
    sums_ref[0:1, :] += jnp.sum(gn * gs, axis=0, keepdims=True)
    h = gn * gain
    dg = scale * (h - gs * jnp.mean(h * gs, axis=1, keepdims=True))
    dy_b = (dg * silu).astype(BF16)
    dy = dy_b.astype(F32)
    dy_ref[0] = dy_b
    dz_ref[0] = (dg * y * (sig + silu * (1.0 - sig))).astype(BF16)
    sums_ref[1:2, :] += jnp.sum(dy * x, axis=0, keepdims=True)
    rows = dy * y_loc
    high = rows.astype(BF16)
    rest = (rows - high.astype(F32)).astype(BF16)
    rows_ref[0] = nn(high, red_ref[...]) + nn(rest, red_ref[...])
    q2_ref[0] = nn((dy * y_in).astype(BF16), red_ref[...])
    ds_ref[0] += tn(cmat, (dy * ece).astype(BF16))


def gate_call(y, act, z, dev, s_in, u, cot, w_out, vecs, ex, red, rows):
    seqs, length, inner = y.shape
    width = act.shape[2]
    depth = u.shape[2]
    whole = lambda s, c: (0, 0)
    row = lambda s, c: (s, c, 0)
    per_seq = lambda s, c: (s, 0, 0)
    lanes = jax.ShapeDtypeStruct((seqs, length, LANES), F32)
    wide = jax.ShapeDtypeStruct((seqs, length, inner), BF16)
    return pl.pallas_call(
        gate_kernel,
        grid=(seqs, length // rows),
        in_specs=[
            pl.BlockSpec((1, rows, inner), row),
            pl.BlockSpec((1, rows, width), row),
            pl.BlockSpec((1, rows, inner), row),
            pl.BlockSpec((1, rows, LANES), row),
            pl.BlockSpec((1, STATE, inner), per_seq),
            pl.BlockSpec((1, rows, depth), row),
            pl.BlockSpec((1, rows, depth), row),
            pl.BlockSpec(w_out.shape, whole),
            pl.BlockSpec(vecs.shape, whole),
            pl.BlockSpec(ex.shape, whole),
            pl.BlockSpec(red.shape, whole),
        ],
        out_specs=[
            pl.BlockSpec((1, rows, depth), row),
            pl.BlockSpec((1, rows, inner), row),
            pl.BlockSpec((1, rows, inner), row),
            pl.BlockSpec((1, rows, inner), row),
            pl.BlockSpec((1, rows, LANES), row),
            pl.BlockSpec((1, rows, LANES), row),
            pl.BlockSpec((8, inner), whole),
            pl.BlockSpec((1, STATE, inner), per_seq),
        ],
        out_shape=[
            jax.ShapeDtypeStruct((seqs, length, depth), BF16),
            wide,
            wide,
            wide,
            lanes,
            lanes,
            jax.ShapeDtypeStruct((8, inner), F32),
            jax.ShapeDtypeStruct((seqs, STATE, inner), F32),
        ],
        compiler_params=pltpu.CompilerParams(vmem_limit_bytes=VMEM_LIMIT),
        name="gate_and_output",
    )(y, act, z, dev, s_in, u, cot, w_out, vecs, ex, red)


def back_kernel(
    act_ref, dy_ref, dt_ref, cum_ref, dev_ref, st_ref, sin_ref, rows_ref, vec_ref, ex_ref, red_ref,
    g_ref, direct_ref, da_ref,
    ds_ref,
):
    inner = dy_ref.shape[2]

    @pl.when(pl.program_id(1) == 0)
    def _():
        ds_ref[...] = jnp.zeros_like(ds_ref)

    bmat = act_ref[0, :, inner : inner + STATE]
    cmat = act_ref[0, :, inner + STATE : inner + 2 * STATE]
    cmat_t = cmat.astype(F32).T.astype(BF16)
    row, col = iotas(Q, Q)
    upper = row <= col
    scores = jnp.where(upper, nt(bmat, cmat), 0.0)
    cum = cum_ref[0]
    cum_t = cum.T
    dt2 = split2(dt_ref[0])
    ec2 = split2(jnp.exp(cum))
    tail2 = split2(jnp.exp(cum[Q - 1 : Q, :] - cum))
    before2 = split2(jnp.exp(dev_ref[0, 0:8, :] - cum[0:8, :]))

    d_scores = jnp.zeros((Q, Q), F32)
    db = jnp.zeros((Q, STATE), F32)
    dc = jnp.zeros((Q, STATE), F32)
    direct = jnp.zeros((Q, LANES), F32)
    col_sums = jnp.zeros((Q, LANES), F32)
    w_loc = jnp.zeros((Q, LANES), F32)
    const = jnp.zeros((8, LANES), F32)
    for quad in range(inner // QUAD):
        cols = slice(quad * QUAD, (quad + 1) * QUAD)
        ex = ex_ref[:, cols]
        red = red_ref[cols, :]
        dte = nn(dt2, ex)
        tle = nn(tail2, ex)
        ece = nn(ec2, ex)
        x = act_ref[0, :, cols].astype(F32)
        xdt_b = (x * dte).astype(BF16)
        xdt = xdt_b.astype(F32)
        dy_b = dy_ref[0, :, cols]
        dy = dy_b.astype(F32)
        parts = []
        for pair in range(2):
            lanes = slice(pair * LANES, (pair + 1) * LANES)
            stacked = block_pair(dy_b[:, lanes])
            d_mat = nt(xdt_b[:, lanes], stacked)
            mats = []
            for j in range(2):
                h = quad * 4 + pair * 2 + j
                decay = jnp.exp(jnp.minimum(cum_t[h : h + 1, :] - cum[:, h : h + 1], 0.0))
                mats.append((scores * decay).astype(BF16))
                d_scores = d_scores + d_mat[:, j * Q : (j + 1) * Q] * decay
            parts.append(nn(jnp.concatenate(mats, axis=1), stacked))
        ds = ds_ref[:, cols]
        ds_b = ds.astype(BF16)
        st = st_ref[0, 0, :, cols].astype(F32)
        before = nn(before2, ex)[0:1, :]
        state_b = (st + before * sin_ref[0, :, cols].astype(F32)).astype(BF16)
        dx_intra = jnp.concatenate(parts, axis=1)
        dx_inter = tle * nn(bmat, ds_b)
        dxp = dx_intra + dx_inter
        g_ref[0, :, cols] = dte * dxp + vec_ref[1:2, cols] * dy
        direct = direct + nn((x * dxp).astype(BF16), red)
        prod = xdt * dx_intra
        high = prod.astype(BF16)
        col_sums = col_sums + nn(high, red) + nn((prod - high.astype(F32)).astype(BF16), red)
        w_loc = w_loc + nn((xdt * dx_inter).astype(BF16), red)
        db = db + nt((xdt * tle).astype(BF16), ds_b)
        dye = (dy * ece).astype(BF16)
        dc = dc + nt(dye, state_b)
        last = ece[Q - 1 : Q, :]
        both = jnp.sum(st * ds, axis=0, keepdims=True) * last
        both = jnp.broadcast_to(both, (8, QUAD))
        high = both.astype(BF16)
        const = const + nn(high, red) + nn((both - high.astype(F32)).astype(BF16), red)
        ds_ref[:, cols] = ds * last + nn(cmat_t, dye)
    d_scores = jnp.where(upper, d_scores, 0.0)
    g_ref[0, :, inner : inner + STATE] = db + nn(d_scores.astype(BF16), cmat)
    g_ref[0, :, inner + STATE :] = dc + nn(d_scores.T.astype(BF16), bmat)
    direct_ref[0] = direct
    da_ref[0] = (
        exact(upper.astype(F32), rows_ref[0] - col_sums)
        + exact((row > col).astype(F32), w_loc)
        + const[0:1, :]
    )


def back_call(act, dy, dts, cum, dev, states, s_in, rows, vecs, ex, red):
    seqs, length, width = act.shape
    inner = dy.shape[2]
    chunks = length // Q
    whole = lambda s, c: (0, 0)
    row = lambda s, c: (s, chunks - 1 - c, 0)
    lanes = jax.ShapeDtypeStruct((seqs, length, LANES), F32)
    lane_block = pl.BlockSpec((1, Q, LANES), row)
    return pl.pallas_call(
        back_kernel,
        grid=(seqs, chunks),
        in_specs=[
            pl.BlockSpec((1, Q, width), row),
            pl.BlockSpec((1, Q, inner), row),
            lane_block,
            lane_block,
            lane_block,
            pl.BlockSpec((1, 1, STATE, inner), lambda s, c: (s, chunks - 1 - c, 0, 0)),
            pl.BlockSpec((1, STATE, inner), lambda s, c: (s, 0, 0)),
            lane_block,
            pl.BlockSpec(vecs.shape, whole),
            pl.BlockSpec(ex.shape, whole),
            pl.BlockSpec(red.shape, whole),
        ],
        out_specs=[pl.BlockSpec((1, Q, width), row), lane_block, lane_block],
        out_shape=[jax.ShapeDtypeStruct((seqs, length, width), F32), lanes, lanes],
        scratch_shapes=[pltpu.VMEM((STATE, inner), F32)],
        compiler_params=pltpu.CompilerParams(vmem_limit_bytes=VMEM_LIMIT),
        name="scan_backward",
    )(act, dy, dts, cum, dev, states, s_in, rows, vecs, ex, red)


def finish_kernel(
    g_ref, act_ref, xbc_ref, prev_ref, halo_ref, raw_ref, dt_ref, dev_ref, tot_ref, ds_ref, q2_ref,
    direct_ref, da_ref, c4_ref, taps_ref, bias_ref, heads_ref, ex_ref, red_ref,
    gconv_ref, gdt_ref, taps_sum_ref, heads_sum_ref,
    ext_ref, carry_ref,
):
    s, c = pl.program_id(0), pl.program_id(1)
    width = xbc_ref.shape[2]
    inner = ds_ref.shape[2]
    rows = xbc_ref.shape[1]

    @pl.when(jnp.logical_and(s == 0, c == 0))
    def _():
        taps_sum_ref[...] = jnp.zeros_like(taps_sum_ref)
        heads_sum_ref[...] = jnp.zeros_like(heads_sum_ref)

    @pl.when(c == 0)
    def _():
        carry_ref[...] = jnp.zeros_like(carry_ref)

    fill_ext(ext_ref, xbc_ref, prev_ref, halo_ref, c == 0)

    def conv_back(grad, cols):
        conv = conv_columns(ext_ref, taps_ref, bias_ref, cols, rows)
        sig = sigmoid(conv)
        out = grad * (sig + conv * sig * (1.0 - sig))
        gconv_ref[0, :, cols] = out
        for k in range(4):
            taps_sum_ref[k : k + 1, cols] += jnp.sum(
                out * ext_ref[pl.ds(5 + k, rows), cols], axis=0, keepdims=True
            )
        taps_sum_ref[4:5, cols] += jnp.sum(out, axis=0, keepdims=True)

    bmat = act_ref[0, :, inner : inner + STATE]
    dts = dt_ref[0]
    dt2 = split2(dts)
    tail2 = split2(jnp.exp(tot_ref[0, 0:1, :] - dev_ref[0]))
    db = jnp.zeros((rows, STATE), F32)
    direct = direct_ref[0]
    q3 = jnp.zeros((rows, LANES), F32)
    for quad in range(inner // QUAD):
        cols = slice(quad * QUAD, (quad + 1) * QUAD)
        ex = ex_ref[:, cols]
        red = red_ref[cols, :]
        dte = nn(dt2, ex)
        tle = nn(tail2, ex)
        x = act_ref[0, :, cols].astype(F32)
        xdt = (x * dte).astype(BF16).astype(F32)
        ds_b = ds_ref[0, :, cols]
        dxc = tle * nn(bmat, ds_b)
        direct = direct + nn((x * dxc).astype(BF16), red)
        q3 = q3 + nn((xdt * dxc).astype(BF16), red)
        db = db + nt((xdt * tle).astype(BF16), ds_b)
        conv_back(g_ref[0, :, cols] + dte * dxc, cols)
    db_all = jnp.concatenate([db, jnp.zeros_like(db)], axis=1)
    cols = slice(inner, inner + QUAD)
    conv_back(g_ref[0, :, cols] + db_all, cols)

    step = q3 - q2_ref[0]
    row, col = iotas(rows, rows)
    prefix = exact((row > col).astype(F32), step) + carry_ref[0:1, :]
    carry_ref[...] = carry_ref[...] + jnp.sum(step, axis=0, keepdims=True)
    da = da_ref[0] + c4_ref[0, 0:1, :] + prefix
    rate = heads_ref[1:2, :]
    raw = raw_ref[0].astype(F32) + heads_ref[0:1, :]
    grad = (direct + rate * da) * sigmoid(raw) * heads_ref[3:4, :]
    gdt_ref[0] = grad.astype(BF16)
    heads_sum_ref[0:1, :] += jnp.sum(grad, axis=0, keepdims=True)
    heads_sum_ref[1:2, :] += jnp.sum(da * dts, axis=0, keepdims=True) * rate


def finish_call(
    grad, act, xbc, halo, raw, dts, dev, tot, ds_end, q2, direct, da, c4, taps, bias, heads, ex, red,
    rows,
):
    seqs, length, width = xbc.shape
    inner = ds_end.shape[2]
    whole = lambda s, c: (0, 0)
    row = lambda s, c: (s, c, 0)
    per_seq = lambda s, c: (s, 0, 0)
    lane_block = pl.BlockSpec((1, rows, LANES), row)
    wide_block = pl.BlockSpec((1, rows, width), row)
    return pl.pallas_call(
        finish_kernel,
        grid=(seqs, length // rows),
        in_specs=[
            wide_block,
            wide_block,
            wide_block,
            pl.BlockSpec((1, 16, width), lambda s, c: (s, jnp.maximum(c * (rows // 16) - 1, 0), 0)),
            pl.BlockSpec((1, 16, width), per_seq),
            lane_block,
            lane_block,
            lane_block,
            pl.BlockSpec((1, 8, LANES), per_seq),
            pl.BlockSpec((1, STATE, inner), per_seq),
            lane_block,
            lane_block,
            lane_block,
            pl.BlockSpec((1, 8, LANES), per_seq),
            pl.BlockSpec(taps.shape, whole),
            pl.BlockSpec(bias.shape, whole),
            pl.BlockSpec(heads.shape, whole),
            pl.BlockSpec(ex.shape, whole),
            pl.BlockSpec(red.shape, whole),
        ],
        out_specs=[
            wide_block,
            lane_block,
            pl.BlockSpec((8, width), whole),
            pl.BlockSpec((8, LANES), whole),
        ],
        out_shape=[
            jax.ShapeDtypeStruct((seqs, length, width), F32),
            jax.ShapeDtypeStruct((seqs, length, LANES), BF16),
            jax.ShapeDtypeStruct((8, width), F32),
            jax.ShapeDtypeStruct((8, LANES), F32),
        ],
        scratch_shapes=[pltpu.VMEM((rows + 8, width), F32), pltpu.VMEM((8, LANES), F32)],
        compiler_params=pltpu.CompilerParams(vmem_limit_bytes=VMEM_LIMIT),
        name="conv_backward",
    )(
        grad, act, xbc, xbc, halo, raw, dts, dev, tot, ds_end, q2, direct, da, c4, taps, bias, heads,
        ex, red,
    )


def rms_gain(values, gain):
    return values * lax.rsqrt(jnp.mean(values * values, axis=-1, keepdims=True) + EPS) * gain


def shift_in(value, size, step):
    pairs = [(i, i + step) for i in range(size) if 0 <= i + step < size]
    return lax.ppermute(value, "seq", pairs)


def carry_over(states, totals, size, step):
    seqs, depth, inner = states.shape
    piece = depth // size
    sent = states.astype(BF16).reshape(seqs, size, piece, inner)
    got = lax.all_to_all(sent, "seq", split_axis=1, concat_axis=1, tiled=True).astype(F32)
    decay = jnp.exp(lax.all_gather(totals, "seq", axis=0))
    order = range(size) if step > 0 else range(size - 1, -1, -1)
    held = jnp.zeros((seqs, piece, inner), F32)
    into = [None] * size
    for i in order:
        into[i] = held
        held = held * decay[i][:, None, :] + got[:, i]
    back = jnp.stack(into, axis=1).astype(BF16)
    back = lax.all_to_all(back, "seq", split_axis=1, concat_axis=1, tiled=True)
    return back.reshape(seqs, depth, inner)


def body(
    size, inputs, w_in, w_out, norm_gain, conv_weight, conv_bias, dt_bias, a_log, skip, gate_gain,
    cotangent,
):
    seqs, length, depth = inputs.shape
    inner = gate_gain.shape[0]
    width = conv_weight.shape[1]
    tokens = seqs * length
    rows = min(256, length)

    full_in = lax.all_gather(w_in, "seq", axis=0, tiled=True)
    full_out = lax.all_gather(w_out, "seq", axis=0, tiled=True)
    w_z = full_in[:, :inner]
    w_x = full_in[:, inner : inner + width]
    w_dt = jnp.pad(full_in[:, inner + width :], ((0, 0), (0, LANES - HEADS)))

    def pad_heads(values):
        return jnp.pad(values, (0, LANES - HEADS))

    rates = -jnp.exp(a_log)
    heads = jnp.stack([pad_heads(dt_bias), pad_heads(rates), pad_heads(skip), pad_heads(jnp.ones_like(skip))])
    heads = jnp.pad(heads, ((0, 4), (0, 0)))
    taps = jnp.pad(conv_weight, ((0, 4), (0, 0)))
    bias = jnp.pad(conv_bias[None, :], ((0, 7), (0, 0)))
    vecs = jnp.pad(jnp.stack([gate_gain, jnp.repeat(skip, HEADDIM)]), ((0, 6), (0, 0)))
    ex, red = head_matrices(inner)

    edge = shift_in(inputs[:, length - 16 :], size, 1).astype(F32)
    halo = jnp.dot(rms_gain(edge, norm_gain).astype(BF16).reshape(seqs * 16, depth), w_x,
                   preferred_element_type=F32).astype(BF16).reshape(seqs, 16, width)
    u = inputs.reshape(tokens, depth)
    u32 = u.astype(F32)
    scale = lax.rsqrt(jnp.mean(u32 * u32, axis=-1, keepdims=True) + EPS)
    normed = (u32 * scale * norm_gain).astype(BF16)

    def project(matrix):
        out = jnp.dot(normed, matrix, preferred_element_type=F32).astype(BF16)
        return out.reshape(seqs, length, matrix.shape[1])

    xbc, raw, z = project(w_x), project(w_dt), project(w_z)

    act, y, dts, cum, dev, states, final = scan_call(xbc, halo, raw, taps, bias, heads, ex, inner)
    total = dev[:, length - 1, :]
    total_cols = jnp.repeat(total[:, :HEADS], HEADDIM, axis=1)
    s_in = carry_over(final, total_cols, size, 1)

    mixed, dy, dz, normalized, row_sums, q2, gate_sums, ds_loc = gate_call(
        y, act, z, dev, s_in, inputs, cotangent, full_out, vecs, ex, red, rows
    )
    cot = cotangent.reshape(tokens, depth)
    grad_out_full = lax.dot_general(
        normalized.reshape(tokens, inner), cot, (((0,), (0,)), ((), ())), preferred_element_type=F32
    )
    rows_out = lax.psum(lax.psum_scatter(grad_out_full, "seq", scatter_dimension=0, tiled=True), "dp")

    ds_end = carry_over(ds_loc, total_cols, size, -1)
    grad, direct, da = back_call(act, dy, dts, cum, dev, states, s_in, row_sums, vecs, ex, red)

    both = (s_in.astype(F32) * ds_end.astype(F32)).sum(axis=1).reshape(seqs, HEADS, HEADDIM).sum(axis=2)
    both = jnp.pad(both, ((0, 0), (0, LANES - HEADS))) * jnp.exp(total)
    c4 = jnp.broadcast_to((both + q2.sum(axis=1))[:, None, :], (seqs, 8, LANES))
    tot = jnp.broadcast_to(total[:, None, :], (seqs, 8, LANES))
    gconv, gdt, taps_sum, heads_sum = finish_call(
        grad, act, xbc, halo, raw, dts, dev, tot, ds_end, q2, direct, da, c4, taps, bias, heads, ex,
        red, rows,
    )

    after = shift_in(gconv[:, :8], size, -1)
    ext = jnp.concatenate([gconv, after], axis=1)
    gx = sum(conv_weight[k][None, None, :] * ext[:, 3 - k : 3 - k + length] for k in range(4))
    gx = gx.astype(BF16).reshape(tokens, width)
    dz = dz.reshape(tokens, inner)
    gdt = gdt.reshape(tokens, LANES)

    def weight_grad(columns):
        return lax.dot_general(normed, columns, (((0,), (0,)), ((), ())), preferred_element_type=F32)

    grad_in_full = jnp.concatenate(
        [weight_grad(dz), weight_grad(gx), weight_grad(gdt)[:, :HEADS]], axis=1
    )
    rows_in = lax.psum(lax.psum_scatter(grad_in_full, "seq", scatter_dimension=0, tiled=True), "dp")

    grad_normed = sum(
        lax.dot_general(columns, matrix, (((1,), (1,)), ((), ())), preferred_element_type=F32)
        for columns, matrix in ((dz, w_z), (gx, w_x), (gdt, w_dt))
    )
    us = u32 * scale
    h = grad_normed * norm_gain
    grad_norm_gain = jnp.sum(grad_normed * us, axis=0)
    grad_u = scale * (h - us * jnp.mean(h * us, axis=-1, keepdims=True))
    grad_inputs = (cot.astype(F32) + grad_u).reshape(seqs, length, depth)

    sums = lax.psum(
        (
            grad_norm_gain,
            taps_sum[:4],
            taps_sum[4],
            heads_sum[0, :HEADS],
            heads_sum[1, :HEADS],
            gate_sums[1].reshape(HEADS, HEADDIM).sum(axis=1),
            gate_sums[0],
        ),
        ("dp", "seq"),
    )
    return (mixed, grad_inputs, rows_in, rows_out, *sums)


def solution(mesh):
    placed = (
        P("dp", "seq", None),
        P("seq", None),
        P("seq", None),
        P(),
        P(),
        P(),
        P(),
        P(),
        P(),
        P(),
        P("dp", "seq", None),
    )
    return jax.shard_map(
        functools.partial(body, mesh.shape["seq"]),
        mesh=mesh,
        in_specs=placed,
        out_specs=(
            P("dp", "seq", None),
            P("dp", "seq", None),
            P("seq", None),
            P("seq", None),
            P(),
            P(),
            P(),
            P(),
            P(),
            P(),
            P(),
        ),
        check_vma=False,
    )
```

time: 4240 us -> 723 us (0.17)
  local copies, waits for them, and re-layouts: 1340 us -> 38.8 us
  waiting for transfers between devices: 1350 us -> 238 us
  matrix products: 977 us -> 72.1 us
  other arithmetic: 428 us -> 64.8 us
  Pallas kernels: 0 us -> 185 us
    all_to_all x8 -> x4, waiting for transfers between devices: 1110 us -> 2.74 us  [the longest x2 2.73 us: carry_over(): back = lax.all_to_all(back, 'seq', split_axis=1, concat_axis=1, tiled=True)]
    dot_general x1094 -> x11, matrix products: 977 us -> 72.1 us  [the longest x3 22.6 us: body(): lax.dot_general(columns, matrix, (((1,), (1,)), ((), ())), preferred_elem...]
    dynamic_update_slice x322 -> x0, local copies, waits for them, and re-layouts: 743 us -> none  [the longest x320 742 us: scan_heads(): final, outs = lax.scan(jax.checkpoint(span_step), start, blocks)]
    squeeze x320 -> x1, local copies, waits for them, and re-layouts: 227 us -> 0.84 us  [body(): heads_sum[1, :HEADS]]
    pallas_call x0 -> x4, Pallas kernels: none -> 185 us  [the longest x1 58.8 us: back_call(): pl.pallas_call(back_kernel, grid=(seqs, chunks), in_specs=[pl.BlockSpec((...]
    mul x131 -> x0, other arithmetic: 129 us -> none  [the longest x1 64.3 us: head_block(): mixed_in = jax.nn.silu(causal_conv(signal, taps, offset))]
    reduce_sum x198 -> x5, other arithmetic: 124 us -> 5.94 us  [the longest x1 2.58 us: body(): scale = lax.rsqrt(jnp.mean(u32 * u32, axis=-1, keepdims=True) + EPS)]
    dynamic_slice x68 -> x0, local copies, waits for them, and re-layouts: 99.9 us -> none  [the longest x64 98.9 us: scan_heads(): final, outs = lax.scan(jax.checkpoint(span_step), start, blocks)]
  transfers between devices with their start and end apart: 13 -> 11, of which waited for: 10 -> 5; matrix products, arithmetic and copies ran while one was open for 8% -> 23% of each run, Pallas kernels for 0% -> 20%
where the time goes in v1:
time: 723 us; the launch traced here: 714 us
  waiting for transfers between devices  238 us (33%)
  Pallas kernels  185 us (26%)
  blocking collectives  72.8 us (10%)
  matrix products  72.1 us (10%)
  other arithmetic  64.8 us (9%)
  local copies, waits for them, and re-layouts  38.8 us (5%)
  starting transfers between devices  28.2 us (4%)
  between operations  14.3 us (2%)
    reduce_scatter x1, waiting for transfers between devices, body(): lax.psum_scatter(grad_in_full, 'seq', scatter_dimension=0, tiled=True)  158 us
    all_gather x1, waiting for transfers between devices, body(): full_in = lax.all_gather(w_in, 'seq', axis=0, tiled=True)  73.4 us
    pallas_call x1, Pallas kernels, back_call(): pl.pallas_call(back_kernel, grid=(seqs, chunks), in_specs=[pl.BlockSpec((...  58.8 us
    pallas_call x1, Pallas kernels, finish_call(): pl.pallas_call(finish_kernel, grid=(seqs, length // rows), in_specs=[wide...  44 us
    psum x1, blocking collectives, body(): lax.psum((grad_norm_gain, taps_sum[:4], taps_sum[4], heads_sum[0, :HEADS]...  41.4 us
    pallas_call x1, Pallas kernels, gate_call(): pl.pallas_call(gate_kernel, grid=(seqs, length // rows), in_specs=[pl.Blo...  41.4 us
    pallas_call x1, Pallas kernels, scan_call(): pl.pallas_call(scan_kernel, grid=(seqs, chunks), in_specs=[pl.BlockSpec((...  40.9 us
    all_gather x1, blocking collectives, carry_over(): decay = jnp.exp(lax.all_gather(totals, 'seq', axis=0))  31.4 us
  transfers between devices with their start and end apart: 11, of which 5 were waited for; matrix products, arithmetic and copies ran while one was open for 23% of the time, Pallas kernels for 20%

profile of v1, /device:TPU:0, one launch (start us, length us, event | category | flops | bytes accessed | tf_op | source)
XLA Modules:
  0.0 714.4 jit_solution(12403730047757944835)
XLA Ops:
  8.9 4.8 collective-permute-start
  26.6 73.4 %all-gather.3.cloned.1.call-done = bf16[768,3352]{1,0:T(8,128)(2,1)} async-done(((bf16[96,3352]{1,0:T(8,128)(2,1)}), bf16[768,3352]{1,0:T(8,128)(2,1)}) %all-gather.3.cloned.1.call-update) | async-done | bytes 5148688 | tf_op jit(solution)/shard_map/all_gather | solution.py:586
  103.7 8.1 %fusion.14.xbc_ref.prev_ref = bf16[1,2048,1792]{2,1,0:T(8,128)(2,1)} fusion(bf16[768,3352]{1,0:T(8,128)(2,1)S(1)} %bitcast.113, bf16[1,2048,768]{2,1,0:T(8,128)(2,1)S(1)} %copy-done, f32[768]{0:T(1024)S(1)} %copy-done.16, f32[2048]{0:T(1024)S(1)} %add_rsqrt_fusion), kind=kOutput, calls=%fused_computation.22 | convolution fusion | flops 5647106048 | bytes 13250560 | tf_op jit(solution)/shard_map/dot_general | solution.py:612
  112.9 40.9 %scan_forward.1 = (bf16[1,2048,1792]{2,1,0:T(8,128)(2,1)}, f32[1,2048,1536]{2,1,0:T(8,128)}, f32[1,2048,128]{2,1,0:T(8,128)}, f32[1,2048,128]{2,1,0:T(8,128)}, f...) custom-call(bf16[1,2048,1792]{2,1,0:T(8,128)(2,1)} %fusion.14.xbc_ref.prev_ref, ...), custom_call_target="tpu_custom_call" | custom-call | tf_op jit(solution)/shard_map/scan_forward/pallas_call | solution.py:162
  155.8 3.5 all-to-all-start
  162.8 31.4 %all_gather.11 = f32[8,1,1536]{2,1,0:T(1,128)S(1)} all-gather(f32[1,1,1536]{2,1,0:T(1,128)} %broadcast_in_dim.36), channel_id=1, replica_groups=mesh['dp'=4,'seq'=8] {'seq'}, dimensions={0}, use_global_device_ids=true | all-gather | bytes 55296 | tf_op jit(solution)/shard_map/all_gather | solution.py:564
  204.3 5.5 all-to-all-start.1
  209.9 8.8 %fusion.15.z_ref = bf16[1,2048,1536]{2,1,0:T(8,128)(2,1)} fusion(bf16[768,3352]{1,0:T(8,128)(2,1)} %all-gather.3.cloned.1.call-done, bf16[1,2048,768]{2,1,0:T(8,128)(2,1)S(1)} %copy-done, f32[768]{0:T(1024)} %param.14, f32[2048]{0:T(1024)} %copy-done.13), kind=kOutput, calls=%fused_computation.23 | convolution fusion | flops 4841275392 | bytes 11808768 | tf_op jit(solution)/shard_map/dot_general | solution.py:612
  219.8 41.4 %gate_and_output.1 = (bf16[1,2048,768]{2,1,0:T(8,128)(2,1)}, bf16[1,2048,1536]{2,1,0:T(8,128)(2,1)}, bf16[1,2048,1536]{2,1,0:T(8,128)(2,1)}, bf16[1,2048,1536]{2...) custom-call(f32[1,2048,1536]{2,1,0:T(8,128)} %get-tuple-element.33.y, ...), custom_call_target="tpu_custom_call" | custom-call | tf_op jit(solution)/shard_map/gate_and_output/pallas_call | solution.py:261
  263.1 5.6 all-to-all-start.2
  271.0 8.6 %fusion.26 = f32[1536,768]{1,0:T(8,128)} fusion(bf16[1,2048,1536]{2,1,0:T(8,128)(2,1)} %get-tuple-element.51, bf16[1,2048,768]{2,1,0:T(8,128)(2,1)S(1)} %copy-done.2), kind=kOutput, calls=%fused_computation.34 | convolution fusion | flops 4831838208 | bytes 14155776 | tf_op jit(solution)/shard_map/dot_general | solution.py:626
  279.7 58.8 %scan_backward.1 = (f32[1,2048,1792]{2,1,0:T(8,128)}, f32[1,2048,128]{2,1,0:T(8,128)}, f32[1,2048,128]{2,1,0:T(8,128)}) custom-call(bf16[1,2048,1792]{2,1,0:T(8,128)(2,1)} %get-tuple-element.34.act_ref, bf16[1,2048,1536]{2,1,0:T(8,128)(2,1)} %get-tuple-element.39.dy_ref, f32[1,2048,128]{2,1,0:T(8,128)} %get-tuple-element.40.dt_ref, ...), custom_call_target="tpu_custom_call" | custom-call | tf_op jit(solution)/shard_map/scan_backward/pallas_call | solution.py:399
  345.1 6.0 all-to-all-start.3
  351.7 10.2 %fusion.28 = f32[768,1536]{1,0:T(8,128)} fusion(bf16[1,2048,1536]{2,1,0:T(8,128)(2,1)} %get-tuple-element.38, bf16[1,2048,768]{2,1,0:T(8,128)(2,1)S(1)} %copy-done.1, f32[768]{0:T(1024)} %param.14, f32[2048]{0:T(1024)} %copy-done.13), kind=kOutput, calls=%fused_computation.36 | convolution fusion | flops 4838129664 | bytes 14167040 | tf_op jit(solution)/shard_map/dot_general | solution.py:651
  367.5 44.0 %conv_backward.1 = (f32[1,2048,1792]{2,1,0:T(8,128)}, bf16[1,2048,128]{2,1,0:T(8,128)(2,1)}, f32[8,1792]{1,0:T(8,128)}, f32[8,128]{1,0:T(8,128)}) custom-call(f32[1,2048,1792]{2,1,0:T(8,128)} %get-tuple-element.44.g_ref, bf16[1,2048,1792]{2,1,0:T(8,128)(2,1)} %get-tuple-element.34.act_ref, bf16[1,2048,1792]{2,1,0:T(8,128)(2,1)} %fusion.14.xbc_ref.prev_ref, ...), custom_call_target="tpu_custom_call" | custom-call | tf_op jit(solution)/shard_map/conv_backward/pallas_call | solution.py:505
  413.9 11.3 %constant_dynamic-update-slice_fusion.3 = f32[1,2056,1792]{2,1,0:T(8,128)} fusion(f32[1,2048,1792]{2,1,0:T(8,128)} %get-tuple-element.49), kind=kLoop, calls=%fused_computation.104 | loop fusion | bytes 29360128
  428.4 19.7 %fusion.2 = bf16[1,2048,1792]{2,1,0:T(8,128)(2,1)S(1)} fusion(f32[1,2056,1792]{2,1,0:T(8,128)} %constant_dynamic-update-slice_fusion.2, f32[1,2048,1792]{2,1,0:T(8,128)} %get-tuple-element.49, f32[1792]{0:T(1024)S(1)} %copy-done.11, f32[1792]{0:T(1024)S(1)} %copy-done.12, f32[1792]{0:T(1024)S(1)} %copy-done.10, f32[1792]{0:T(1024)S(1)} %copy-done.9), kind=kLoop, calls=%fused_computation.3 | loop fusion | flops 29360128 | bytes 66088960 | tf_op jit(solution)/shard_map/convert_element_type | solution.py:646
  451.1 8.3 %fusion.10 = f32[768,1792]{1,0:T(8,128)} fusion(bf16[1,2048,1792]{2,1,0:T(8,128)(2,1)S(1)} %fusion.2, bf16[1,2048,768]{2,1,0:T(8,128)(2,1)S(1)} %copy-done.1, f32[768]{0:T(1024)S(1)} %copy-done.17, f32[2048]{0:T(1024)S(1)} %copy-done.14), kind=kOutput, calls=%fused_computation.18 | convolution fusion | flops 5643436032 | bytes 16002048 | tf_op jit(solution)/shard_map/dot_general | solution.py:651
  459.4 8.7 %pad_maximum_fusion = f32[768,3352]{1,0:T(8,128)} fusion(f32[768,24]{1,0:T(8,128)S(1)} %fusion.44, f32[768,1792]{1,0:T(8,128)} %fusion.10, f32[768,1536]{1,0:T(8,128)} %fusion.28), kind=kLoop, calls=%fused_computation.7 | loop fusion | flops 5148672 | bytes 20594688 | tf_op jit(solution)/shard_map/concatenate | solution.py:653
  469.5 9.6 %fusion.30 = f32[2048,768]{1,0:T(8,128)} fusion(bf16[1,2048,1536]{2,1,0:T(8,128)(2,1)} %get-tuple-element.38, bf16[768,3352]{1,0:T(8,128)(2,1)} %all-gather.3.cloned.1.call-done), kind=kOutput, calls=%fused_computation.38 | convolution fusion | flops 4831838208 | bytes 14942208 | tf_op jit(solution)/shard_map/dot_general | solution.py:659
  482.1 12.0 %fusion.22 = (f32[768]{0:T(1024)S(1)}, f32[2048]{0:T(1024)S(1)}, f32[2048,768]{1,0:T(8,128)}) fusion(bf16[1,2048,768]{2,1,0:T(8,128)(2,1)S(1)} %copy-done.1, f32[2048]{0:T(1024)S(1)} %copy-done.14, f32[768]{0:T(1024)S(1)} %copy-done.17, f32[2048,768]{1,0:T(8,128)S(1)} %fusion.46, f32[2048,768]{1,0:T(8,128)} %fusion.30, bf16[768,3352]{1,0:T(8,128)(2,1)S(1)} %bitcast.115, ...), kind=kOutput, calls=%fused_computation.30 | convolution fusion | flops 5651297280 | bytes 32136192 | tf_op jit(solution)/shard_map/dot_general | solution.py:659
  494.0 158.0 %reduce-scatter.3.cloned.1.call-done = f32[96,3352]{1,0:T(8,128)} async-done(((f32[768,3352]{1,0:T(8,128)}), f32[96,3352]{1,0:T(8,128)}) %reduce-scatter.3.cloned.1.call-update) | async-done | bytes 1287184 | tf_op jit(solution)/shard_map/reduce_scatter | solution.py:656
  652.1 41.4 %all-reduce.10 = (f32[768]{0:T(1024)}, f32[4,1792]{1,0:T(4,128)}, f32[1792]{0:T(1024)}, f32[24]{0:T(128)}, f32[24]{0:T(128)}, /*index=5*/f32[24]{0:T(128)}, f32[1536]{0:T(1024)}) all-reduce(f32[768]{0:T(1024)S(1)} %get-tuple-element.55, f32[4,1792]{1,0:T(4,128)S(1)} %slice.175, ...), channel_id=1, replica_groups=mesh['dp'=4,'seq'=8] {'dp','seq'}, use_global_device_ids=true, to_apply=%region_11.12 | all-reduce | flops 11336 | bytes 90688 | tf_op jit(solution)/shard_map/psum | solution.py:668
  693.5 6.4 fusion.21
  (141 shorter events, 73.6 us)
Async XLA Ops:
  7.2 94.6 %copy-start = (bf16[1,2048,768]{2,1,0:T(8,128)(2,1)S(1)}, bf16[1,2048,768]{2,1,0:T(8,128)(2,1)}, u32[]{:S(2)}) copy-start(bf16[1,2048,768]{2,1,0:T(8,128)(2,1)} %u_ref.1) | copy-start | bytes 9437188
  7.2 94.6 %copy-start.16 = (f32[768]{0:T(1024)S(1)}, f32[768]{0:T(1024)}, u32[]{:S(2)}) copy-start(f32[768]{0:T(1024)} %param.14) | copy-start | bytes 9220
  7.2 92.8 %all-gather.3.cloned.1.call-start = ((), (), s32[]{:S(2)}) async-start(), calls=%async_computation.6 | async-start | bytes 5971968 | tf_op jit(solution)/shard_map/all_gather | solution.py:586
  7.9 210.7 %all-gather.5.cloned.1.call-start = ((), (), s32[]{:S(2)}) async-start(), calls=%async_computation.7 | async-start | bytes 2654208 | tf_op jit(solution)/shard_map/all_gather | solution.py:587
  8.9 17.6 %collective-permute-start = (bf16[1,16,768]{2,1,0:T(8,128)(2,1)S(1)}, bf16[1,16,768]{2,1,0:T(8,128)(2,1)S(1)}, u32[]{:S(2)}, u32[]{:S(2)}) collective-permute-start(bf16[1,16,768]{2,1,0:T(8,128)(2,1)S(1)} %slice.138), channel_id=1, source_target_pairs={{0,1},{1,2},{2,3},{3,4},{4,5},{5,6},{6,7},{8,9},{9,10},{10,11},{11... | collective-permute-start | bytes 73736 | tf_op jit(solution)/shard_map/ppermute | solution.py:556
  18.1 85.6 %copy-start.13 = (f32[2048]{0:T(1024)}, f32[2048]{0:T(1024)S(1)}, u32[]{:S(2)}) copy-start(f32[2048]{0:T(1024)S(1)} %add_rsqrt_fusion) | copy-start | bytes 24580
  155.8 39.1 %all-to-all-start = ((bf16[1,8,16,1536]{3,2,0,1:T(8,128)(2,1)}), bf16[1,8,16,1536]{3,2,0,1:T(8,128)(2,1)S(1)}, u32[]{:S(2)}, u32[]{:S(2)}) async-start(bf16[1,8,16,1536]{3,2,0,1:T(8,128)(2,1)} %bitcast.117), calls=%async_computation | async-start | bytes 786432 | tf_op jit(solution)/shard_map/all_to_all | solution.py:563
  204.3 14.7 %all-to-all-start.1 = ((bf16[1,8,16,1536]{3,2,0,1:T(8,128)(2,1)}), bf16[1,8,16,1536]{3,2,0,1:T(8,128)(2,1)S(1)}, u32[]{:S(2)}, u32[]{:S(2)}) async-start(bf16[1,8,16,1536]{3,2,0,1:T(8,128)(2,1)} %fusion.58), calls=%async_computation.1 | async-start | bytes 786432 | tf_op jit(solution)/shard_map/all_to_all | solution.py:572
  219.8 51.2 %copy-start.2 = (bf16[1,2048,768]{2,1,0:T(8,128)(2,1)S(1)}, bf16[1,2048,768]{2,1,0:T(8,128)(2,1)}, u32[]{:S(2)}) copy-start(bf16[1,2048,768]{2,1,0:T(8,128)(2,1)} %c_ref.1) | copy-start | bytes 9437188
  263.1 75.4 %all-to-all-start.2 = ((bf16[1,8,16,1536]{3,2,0,1:T(8,128)(2,1)}), bf16[1,8,16,1536]{3,2,0,1:T(8,128)(2,1)S(1)}, u32[]{:S(2)}, u32[]{:S(2)}) async-start(bf16[1,8,16,1536]{3,2,0,1:T(8,128)(2,1)} %bitcast.118), calls=%async_computation.2 | async-start | bytes 786432 | tf_op jit(solution)/shard_map/all_to_all | solution.py:563
  268.7 225.4 %reduce-scatter.5.cloned.1.call-start = ((), (), s32[]{:S(2)}) async-start(), calls=%async_computation.9 | async-start | bytes 5308416 | tf_op jit(solution)/shard_map/reduce_scatter | solution.py:629
  279.6 72.0 %copy-start.1 = (bf16[1,2048,768]{2,1,0:T(8,128)(2,1)S(1)}, bf16[1,2048,768]{2,1,0:T(8,128)(2,1)}, u32[]{:S(2)}) copy-start(bf16[1,2048,768]{2,1,0:T(8,128)(2,1)} %u_ref.1) | copy-start | bytes 9437188
  345.1 19.1 %all-to-all-start.3 = ((bf16[1,8,16,1536]{3,2,0,1:T(8,128)(2,1)}), bf16[1,8,16,1536]{3,2,0,1:T(8,128)(2,1)}, u32[]{:S(2)}, u32[]{:S(2)}) async-start(bf16[1,8,16,1536]{3,2,0,1:T(8,128)(2,1)} %constant_dynamic-update-slice_fusion.1), calls=%async_computation.3 | async-start | bytes 786432 | tf_op jit(solution)/shard_map/all_to_all | solution.py:572
  351.1 300.9 %reduce-scatter.3.cloned.1.call-start = ((), (), s32[]{:S(2)}) async-start(), calls=%async_computation.8 | async-start | bytes 11943936 | tf_op jit(solution)/shard_map/reduce_scatter | solution.py:656
  351.7 12.6 %copy-start.5 = (bf16[1,8,16,1536]{3,2,0,1:T(8,128)(2,1)S(1)}, bf16[1,8,16,1536]{3,2,0,1:T(8,128)(2,1)}, u32[]{:S(2)}) copy-start(bf16[1,8,16,1536]{3,2,0,1:T(8,128)(2,1)} %copy-done.4) | copy-start | bytes 1179652
  351.7 13.9 %copy-start.18 = (f32[128]{0:T(128)S(1)}, f32[128]{0:T(128)}, u32[]{:S(2)}) copy-start(f32[128]{0:T(128)} %reduce_sum.81) | copy-start | bytes 1540
  351.7 15.2 %copy-start.19 = (f32[128]{0:T(128)S(1)}, f32[128]{0:T(128)}, u32[]{:S(2)}) copy-start(f32[128]{0:T(128)} %get-tuple-element.90) | copy-start | bytes 1540
  412.3 12.9 %copy-start.14 = (f32[2048]{0:T(1024)S(1)}, f32[2048]{0:T(1024)}, u32[]{:S(2)}) copy-start(f32[2048]{0:T(1024)} %copy-done.13) | copy-start | bytes 24580
  412.3 13.0 %copy-start.17 = (f32[768]{0:T(1024)S(1)}, f32[768]{0:T(1024)}, u32[]{:S(2)}) copy-start(f32[768]{0:T(1024)} %param.14) | copy-start | bytes 9220
  412.3 15.5 %collective-permute-start.1 = (f32[1,8,1792]{2,1,0:T(8,128)S(1)}, f32[1,8,1792]{2,1,0:T(8,128)S(1)}, u32[]{:S(2)}, u32[]{:S(2)}) collective-permute-start(f32[1,8,1792]{2,1,0:T(8,128)S(1)} %slice.167), channel_id=1, source_target_pairs={{1,0},{2,1},{3,2},{4,3},{5,4},{6,5},{7,6},{9,8},{10,9},{11,10},{12... | collective-permute-start | bytes 172040 | tf_op jit(solution)/shard_map/ppermute | solution.py:556
  468.1 235.2 %all-reduce.14.cloned.1.call-start = ((), (), s32[]{:S(2)}) async-start(), calls=%async_computation.10 | async-start | bytes 3833856 | tf_op jit(solution)/shard_map/psum | solution.py:656
  469.4 9.7 %copy-start.15 = (f32[8,1792]{1,0:T(8,128)S(1)}, f32[8,1792]{1,0:T(8,128)}, u32[]{:S(2)}) copy-start(f32[8,1792]{1,0:T(8,128)} %get-tuple-element.52) | copy-start | bytes 172036
  469.4 10.5 %copy-start.6 = (bf16[1,2048,128]{2,1,0:T(8,128)(2,1)S(1)}, bf16[1,2048,128]{2,1,0:T(8,128)(2,1)}, u32[]{:S(2)}) copy-start(bf16[1,2048,128]{2,1,0:T(8,128)(2,1)} %get-tuple-element.50) | copy-start | bytes 1572868
  469.5 10.5 %copy-start.8 = (bf16[768,24]{1,0:T(8,128)(2,1)S(1)}, bf16[768,24]{1,0:T(8,128)(2,1)}, u32[]{:S(2)}) copy-start(bf16[768,24]{1,0:T(8,128)(2,1)} %copy-done.7) | copy-start | bytes 110596
  (11 other events, 27.2 us)
Sparse Core Ops, SparseCore 0:
  10.2 89.7 all-gather.2
  102.2 50.2 all-gather.4
  279.8 100.3 reduce-scatter.4
  468.2 183.8 reduce-scatter.2
  654.5 48.7 all-reduce.13

commit v2 on v1

--- a/solution.py
+++ b/solution.py
@@ -17,6 +17,13 @@
 F32 = jnp.float32
 BF16 = jnp.bfloat16
 VMEM_LIMIT = 56 * 1024 * 1024
+
+
+def cost(tokens, per_token_ns):
+    seconds = tokens * per_token_ns * 1e-9
+    return pl.CostEstimate(
+        flops=int(seconds * 1e15), bytes_accessed=int(seconds * 3e12), transcendentals=0
+    )
 
 
 def dot(left, right, dims):
@@ -196,6 +203,7 @@
             pltpu.VMEM((8, LANES), F32),
         ],
         compiler_params=pltpu.CompilerParams(vmem_limit_bytes=VMEM_LIMIT),
+        cost_estimate=cost(seqs * length, 20),
         name="scan_forward",
     )(xbc, xbc, halo, raw, taps, bias, heads, ex)
 
@@ -295,8 +303,44 @@
             jax.ShapeDtypeStruct((seqs, STATE, inner), F32),
         ],
         compiler_params=pltpu.CompilerParams(vmem_limit_bytes=VMEM_LIMIT),
+        cost_estimate=cost(seqs * length, 22),
         name="gate_and_output",
     )(y, act, z, dev, s_in, u, cot, w_out, vecs, ex, red)
+
+
+def weights_kernel(norm_ref, c_ref, n_ref, dz_ref, gwo_ref, gwz_ref):
+    @pl.when(jnp.logical_and(pl.program_id(0) == 0, pl.program_id(1) == 0))
+    def _():
+        gwo_ref[...] = jnp.zeros_like(gwo_ref)
+        gwz_ref[...] = jnp.zeros_like(gwz_ref)
+
+    gwo_ref[...] += tn(norm_ref[0], c_ref[0])
+    gwz_ref[...] += tn(n_ref[0], dz_ref[0])
+
+
+def weights_call(normalized, cot, normed, dz, rows):
+    seqs, length, inner = dz.shape
+    depth = cot.shape[2]
+    whole = lambda s, c: (0, 0)
+    row = lambda s, c: (s, c, 0)
+    return pl.pallas_call(
+        weights_kernel,
+        grid=(seqs, length // rows),
+        in_specs=[
+            pl.BlockSpec((1, rows, inner), row),
+            pl.BlockSpec((1, rows, depth), row),
+            pl.BlockSpec((1, rows, depth), row),
+            pl.BlockSpec((1, rows, inner), row),
+        ],
+        out_specs=[pl.BlockSpec((inner, depth), whole), pl.BlockSpec((depth, inner), whole)],
+        out_shape=[
+            jax.ShapeDtypeStruct((inner, depth), F32),
+            jax.ShapeDtypeStruct((depth, inner), F32),
+        ],
+        compiler_params=pltpu.CompilerParams(vmem_limit_bytes=VMEM_LIMIT),
+        cost_estimate=cost(seqs * length, 8),
+        name="weight_gradients",
+    )(normalized, cot, normed, dz)
 
 
 def back_kernel(
@@ -416,6 +460,7 @@
         out_shape=[jax.ShapeDtypeStruct((seqs, length, width), F32), lanes, lanes],
         scratch_shapes=[pltpu.VMEM((STATE, inner), F32)],
         compiler_params=pltpu.CompilerParams(vmem_limit_bytes=VMEM_LIMIT),
+        cost_estimate=cost(seqs * length, 29),
         name="scan_backward",
     )(act, dy, dts, cum, dev, states, s_in, rows, vecs, ex, red)
 
@@ -540,6 +585,7 @@
         ],
         scratch_shapes=[pltpu.VMEM((rows + 8, width), F32), pltpu.VMEM((8, LANES), F32)],
         compiler_params=pltpu.CompilerParams(vmem_limit_bytes=VMEM_LIMIT),
+        cost_estimate=cost(seqs * length, 21),
         name="conv_backward",
     )(
         grad, act, xbc, xbc, halo, raw, dts, dev, tot, ds_end, q2, direct, da, c4, taps, bias, heads,
@@ -547,8 +593,193 @@
     )
 
 
-def rms_gain(values, gain):
-    return values * lax.rsqrt(jnp.mean(values * values, axis=-1, keepdims=True) + EPS) * gain
+def taps_back_kernel(
+    g_ref, next_ref, after_ref, gdt_ref, normed_ref, taps_ref,
+    gx_ref, gw_ref,
+    ext_ref,
+):
+    s, c = pl.program_id(0), pl.program_id(1)
+    rows, width = g_ref.shape[1], g_ref.shape[2]
+
+    @pl.when(jnp.logical_and(s == 0, c == 0))
+    def _():
+        gw_ref[...] = jnp.zeros_like(gw_ref)
+
+    ext_ref[0:rows, :] = g_ref[0]
+    ext_ref[rows : rows + 8, :] = jnp.where(c == pl.num_programs(1) - 1, after_ref[0], next_ref[0])
+    for start in range(0, width, QUAD):
+        cols = slice(start, start + QUAD)
+        total = taps_ref[3:4, cols] * ext_ref[pl.ds(0, rows), cols]
+        for k in range(3):
+            total = total + taps_ref[k : k + 1, cols] * ext_ref[pl.ds(3 - k, rows), cols]
+        gx_ref[0, :, cols] = total.astype(BF16)
+    gx_ref[0, :, width:] = gdt_ref[0]
+    gw_ref[...] += tn(normed_ref[0], gx_ref[0])
+
+
+def taps_back_call(gconv, after, gdt, normed, taps, rows):
+    seqs, length, width = gconv.shape
+    depth = normed.shape[2]
+    whole = lambda s, c: (0, 0)
+    row = lambda s, c: (s, c, 0)
+    last = length // 8 - 1
+    return pl.pallas_call(
+        taps_back_kernel,
+        grid=(seqs, length // rows),
+        in_specs=[
+            pl.BlockSpec((1, rows, width), row),
+            pl.BlockSpec(
+                (1, 8, width), lambda s, c: (s, jnp.minimum((c + 1) * (rows // 8), last), 0)
+            ),
+            pl.BlockSpec((1, 8, width), lambda s, c: (s, 0, 0)),
+            pl.BlockSpec((1, rows, LANES), row),
+            pl.BlockSpec((1, rows, depth), row),
+            pl.BlockSpec(taps.shape, whole),
+        ],
+        out_specs=[
+            pl.BlockSpec((1, rows, width + LANES), row),
+            pl.BlockSpec((depth, width + LANES), whole),
+        ],
+        out_shape=[
+            jax.ShapeDtypeStruct((seqs, length, width + LANES), BF16),
+            jax.ShapeDtypeStruct((depth, width + LANES), F32),
+        ],
+        scratch_shapes=[pltpu.VMEM((rows + 8, width), F32)],
+        compiler_params=pltpu.CompilerParams(vmem_limit_bytes=VMEM_LIMIT),
+        cost_estimate=cost(seqs * length, 9),
+        name="taps_backward",
+    )(gconv, gconv, after, gdt, normed, taps)
+
+
+def input_kernel(dz_ref, gx_ref, wz_ref, wx_ref, u_ref, c_ref, gain_ref, out_ref, sum_ref):
+    @pl.when(jnp.logical_and(pl.program_id(0) == 0, pl.program_id(1) == 0))
+    def _():
+        sum_ref[...] = jnp.zeros_like(sum_ref)
+
+    grad = nt(dz_ref[0], wz_ref[...]) + nt(gx_ref[0], wx_ref[...])
+    u = u_ref[0].astype(F32)
+    scale = lax.rsqrt(jnp.mean(u * u, axis=1, keepdims=True) + EPS)
+    us = u * scale
+    sum_ref[0:1, :] += jnp.sum(grad * us, axis=0, keepdims=True)
+    h = grad * gain_ref[0:1, :]
+    back = scale * (h - us * jnp.mean(h * us, axis=1, keepdims=True))
+    out_ref[0] = c_ref[0].astype(F32) + back
+
+
+def input_call(dz, gx, w_z, w_x, u, cot, gain, rows):
+    seqs, length, depth = u.shape
+    whole = lambda s, c: (0, 0)
+    row = lambda s, c: (s, c, 0)
+    return pl.pallas_call(
+        input_kernel,
+        grid=(seqs, length // rows),
+        in_specs=[
+            pl.BlockSpec((1, rows, dz.shape[2]), row),
+            pl.BlockSpec((1, rows, gx.shape[2]), row),
+            pl.BlockSpec(w_z.shape, whole),
+            pl.BlockSpec(w_x.shape, whole),
+            pl.BlockSpec((1, rows, depth), row),
+            pl.BlockSpec((1, rows, depth), row),
+            pl.BlockSpec(gain.shape, whole),
+        ],
+        out_specs=[pl.BlockSpec((1, rows, depth), row), pl.BlockSpec((8, depth), whole)],
+        out_shape=[
+            jax.ShapeDtypeStruct((seqs, length, depth), F32),
+            jax.ShapeDtypeStruct((8, depth), F32),
+        ],
+        compiler_params=pltpu.CompilerParams(vmem_limit_bytes=VMEM_LIMIT),
+        cost_estimate=cost(seqs * length, 9),
+        name="input_gradient",
+    )(dz, gx, w_z, w_x, u, cot, gain)
+
+
+def to_all(value, size, axes):
+    copies = jnp.broadcast_to(value[None], (size,) + value.shape)
+    return lax.all_to_all(copies, axes, split_axis=0, concat_axis=0, tiled=True)
+
+
+def other_core(value, sizes):
+    return lax.ppermute(value, "dp", [(i, i ^ 1) for i in range(sizes["dp"])])
+
+
+def both_cores(value, sizes, axis):
+    other = other_core(value, sizes)
+    first = lax.axis_index("dp") % 2 == 0
+    return jnp.where(first, jnp.stack([value, other], axis), jnp.stack([other, value], axis))
+
+
+def core_half(shard):
+    half = shard.shape[0] // 2
+    return lax.dynamic_slice_in_dim(shard, (lax.axis_index("dp") % 2) * half, half, 0)
+
+
+def gather_rows(shard, sizes):
+    got = to_all(core_half(shard), sizes["seq"], "seq").reshape(sizes["seq"], -1, shard.shape[1])
+    return both_cores(got, sizes, 1).reshape(sizes["seq"] * shard.shape[0], shard.shape[1])
+
+
+def gather_later(shards, sizes):
+    columns = max(shard.shape[1] for shard in shards)
+    halves = [core_half(shard).reshape(-1, columns) for shard in shards]
+    got = lax.all_gather(jnp.concatenate(halves, axis=0), "seq", axis=0)
+    other = other_core(got, sizes)
+    first = lax.axis_index("dp") % 2 == 0
+    outs, at = [], 0
+    for shard, half in zip(shards, halves):
+        rows = slice(at, at + half.shape[0])
+        at += half.shape[0]
+        mine, away = got[:, rows], other[:, rows]
+        pair = jnp.where(first, jnp.stack([mine, away], 1), jnp.stack([away, mine], 1))
+        outs.append(pair.reshape(sizes["seq"] * shard.shape[0], shard.shape[1]))
+    return outs
+
+
+def scatter_rows(grads, sizes):
+    size = sizes["seq"]
+    core = lax.axis_index("dp") % 2
+    columns = max(grad.shape[1] for grad in grads)
+    halves = []
+    for grad in grads:
+        parts = grad.reshape(size, 2, -1, grad.shape[1])
+        mine = lax.dynamic_index_in_dim(parts, core, 1, keepdims=False)
+        away = lax.dynamic_index_in_dim(parts, 1 - core, 1, keepdims=False).astype(BF16)
+        half = (mine + other_core(away, sizes).astype(F32)).astype(BF16)
+        halves.append(half.reshape(size, -1, columns))
+    return lax.all_to_all(
+        jnp.concatenate(halves, axis=1), "seq", split_axis=0, concat_axis=0, tiled=True
+    )
+
+
+def add_rows(got, shapes, sizes):
+    total = got.astype(F32).sum(axis=0)
+    step = 2
+    while step < sizes["dp"]:
+        total = total + lax.ppermute(total, "dp", [(i, i ^ step) for i in range(sizes["dp"])])
+        step *= 2
+    pair = both_cores(total, sizes, 0)
+    outs, at = [], 0
+    for rows, columns in shapes:
+        count = rows * columns // (2 * sizes["seq"] * total.shape[1])
+        outs.append(pair[:, at : at + count].reshape(rows // sizes["seq"], columns))
+        at += count
+    return outs
+
+
+def sum_small(values, sizes):
+    flat = jnp.concatenate([value.reshape(-1) for value in values])
+    count = flat.shape[0]
+    flat = jnp.pad(flat, (0, -count % 1024)).reshape(-1, LANES)
+    for axis in ("dp", "seq"):
+        step = 1
+        while step < sizes[axis]:
+            flat = flat + lax.ppermute(flat, axis, [(i, i ^ step) for i in range(sizes[axis])])
+            step *= 2
+    flat = flat.reshape(-1)
+    out, at = [], 0
+    for value in values:
+        out.append(flat[at : at + value.size].reshape(value.shape))
+        at += value.size
+    return out
 
 
 def shift_in(value, size, step):
@@ -556,12 +787,13 @@
     return lax.ppermute(value, "seq", pairs)
 
 
-def carry_over(states, totals, size, step):
+def carry_over(states, decay, size, step, beside):
     seqs, depth, inner = states.shape
     piece = depth // size
     sent = states.astype(BF16).reshape(seqs, size, piece, inner)
-    got = lax.all_to_all(sent, "seq", split_axis=1, concat_axis=1, tiled=True).astype(F32)
-    decay = jnp.exp(lax.all_gather(totals, "seq", axis=0))
+    got = lax.all_to_all(sent, "seq", split_axis=1, concat_axis=1, tiled=True)
+    got, beside = lax.optimization_barrier((got, beside))
+    got = got.astype(F32)
     order = range(size) if step > 0 else range(size - 1, -1, -1)
     held = jnp.zeros((seqs, piece, inner), F32)
     into = [None] * size
@@ -570,24 +802,26 @@
         held = held * decay[i][:, None, :] + got[:, i]
     back = jnp.stack(into, axis=1).astype(BF16)
     back = lax.all_to_all(back, "seq", split_axis=1, concat_axis=1, tiled=True)
-    return back.reshape(seqs, depth, inner)
+    return back.reshape(seqs, depth, inner), beside
+
+
+def rms_gain(values, gain):
+    return values * lax.rsqrt(jnp.mean(values * values, axis=-1, keepdims=True) + EPS) * gain
 
 
 def body(
-    size, inputs, w_in, w_out, norm_gain, conv_weight, conv_bias, dt_bias, a_log, skip, gate_gain,
+    sizes, inputs, w_in, w_out, norm_gain, conv_weight, conv_bias, dt_bias, a_log, skip, gate_gain,
     cotangent,
 ):
+    size = sizes["seq"]
     seqs, length, depth = inputs.shape
     inner = gate_gain.shape[0]
     width = conv_weight.shape[1]
     tokens = seqs * length
     rows = min(256, length)
 
-    full_in = lax.all_gather(w_in, "seq", axis=0, tiled=True)
-    full_out = lax.all_gather(w_out, "seq", axis=0, tiled=True)
-    w_z = full_in[:, :inner]
-    w_x = full_in[:, inner : inner + width]
-    w_dt = jnp.pad(full_in[:, inner + width :], ((0, 0), (0, LANES - HEADS)))
+    w_x = gather_rows(jnp.pad(w_in[:, inner:], ((0, 0), (0, LANES - HEADS))), sizes)
+    w_z, full_out = gather_later([w_in[:, :inner], w_out], sizes)
 
     def pad_heads(values):
         return jnp.pad(values, (0, LANES - HEADS))
@@ -601,34 +835,32 @@
     ex, red = head_matrices(inner)
 
     edge = shift_in(inputs[:, length - 16 :], size, 1).astype(F32)
-    halo = jnp.dot(rms_gain(edge, norm_gain).astype(BF16).reshape(seqs * 16, depth), w_x,
-                   preferred_element_type=F32).astype(BF16).reshape(seqs, 16, width)
-    u = inputs.reshape(tokens, depth)
-    u32 = u.astype(F32)
-    scale = lax.rsqrt(jnp.mean(u32 * u32, axis=-1, keepdims=True) + EPS)
-    normed = (u32 * scale * norm_gain).astype(BF16)
-
-    def project(matrix):
-        out = jnp.dot(normed, matrix, preferred_element_type=F32).astype(BF16)
-        return out.reshape(seqs, length, matrix.shape[1])
-
-    xbc, raw, z = project(w_x), project(w_dt), project(w_z)
-
+    edge = rms_gain(edge, norm_gain).astype(BF16).reshape(seqs * 16, depth)
+    normed = rms_gain(inputs.astype(F32), norm_gain).astype(BF16)
+    flat = normed.reshape(tokens, depth)
+
+    def project(left, matrix):
+        return jnp.dot(left, matrix, preferred_element_type=F32).astype(BF16)
+
+    halo = project(edge, w_x)[:, :width].reshape(seqs, 16, width)
+    xbc = project(flat, w_x[:, :width]).reshape(seqs, length, width)
+    raw = project(flat, w_x[:, width:]).reshape(seqs, length, LANES)
+
+    total = (softplus(raw.astype(F32) + heads[0]) * heads[3]).sum(axis=1) * heads[1]
+    decay = jnp.exp(to_all(total, size, "seq").reshape(size, seqs, LANES)[:, :, :HEADS])
+    decay = jnp.repeat(decay, HEADDIM, axis=2)
     act, y, dts, cum, dev, states, final = scan_call(xbc, halo, raw, taps, bias, heads, ex, inner)
-    total = dev[:, length - 1, :]
-    total_cols = jnp.repeat(total[:, :HEADS], HEADDIM, axis=1)
-    s_in = carry_over(final, total_cols, size, 1)
+    final, decay = lax.optimization_barrier((final, decay))
+    z = project(flat, w_z).reshape(seqs, length, inner)
+    s_in, z = carry_over(final, decay, size, 1, z)
 
     mixed, dy, dz, normalized, row_sums, q2, gate_sums, ds_loc = gate_call(
         y, act, z, dev, s_in, inputs, cotangent, full_out, vecs, ex, red, rows
     )
-    cot = cotangent.reshape(tokens, depth)
-    grad_out_full = lax.dot_general(
-        normalized.reshape(tokens, inner), cot, (((0,), (0,)), ((), ())), preferred_element_type=F32
-    )
-    rows_out = lax.psum(lax.psum_scatter(grad_out_full, "seq", scatter_dimension=0, tiled=True), "dp")
-
-    ds_end = carry_over(ds_loc, total_cols, size, -1)
+    grad_out, grad_z = weights_call(normalized, cotangent, normed, dz, min(512, length))
+    ds_end, weight_grads = carry_over(ds_loc, decay, size, -1, (grad_out, grad_z))
+    got_zo = scatter_rows(weight_grads, sizes)
+
     grad, direct, da = back_call(act, dy, dts, cum, dev, states, s_in, row_sums, vecs, ex, red)
 
     both = (s_in.astype(F32) * ds_end.astype(F32)).sum(axis=1).reshape(seqs, HEADS, HEADDIM).sum(axis=2)
@@ -639,35 +871,16 @@
         grad, act, xbc, halo, raw, dts, dev, tot, ds_end, q2, direct, da, c4, taps, bias, heads, ex,
         red, rows,
     )
-
+    gconv, got_zo = lax.optimization_barrier((gconv, got_zo))
     after = shift_in(gconv[:, :8], size, -1)
-    ext = jnp.concatenate([gconv, after], axis=1)
-    gx = sum(conv_weight[k][None, None, :] * ext[:, 3 - k : 3 - k + length] for k in range(4))
-    gx = gx.astype(BF16).reshape(tokens, width)
-    dz = dz.reshape(tokens, inner)
-    gdt = gdt.reshape(tokens, LANES)
-
-    def weight_grad(columns):
-        return lax.dot_general(normed, columns, (((0,), (0,)), ((), ())), preferred_element_type=F32)
-
-    grad_in_full = jnp.concatenate(
-        [weight_grad(dz), weight_grad(gx), weight_grad(gdt)[:, :HEADS]], axis=1
-    )
-    rows_in = lax.psum(lax.psum_scatter(grad_in_full, "seq", scatter_dimension=0, tiled=True), "dp")
-
-    grad_normed = sum(
-        lax.dot_general(columns, matrix, (((1,), (1,)), ((), ())), preferred_element_type=F32)
-        for columns, matrix in ((dz, w_z), (gx, w_x), (gdt, w_dt))
-    )
-    us = u32 * scale
-    h = grad_normed * norm_gain
-    grad_norm_gain = jnp.sum(grad_normed * us, axis=0)
-    grad_u = scale * (h - us * jnp.mean(h * us, axis=-1, keepdims=True))
-    grad_inputs = (cot.astype(F32) + grad_u).reshape(seqs, length, depth)
-
-    sums = lax.psum(
+    rows_out, rows_z = add_rows(got_zo, [grad_out.shape, grad_z.shape], sizes)
+    gx, grad_x = taps_back_call(gconv, after, gdt, normed, taps, rows)
+    (rows_x,) = add_rows(scatter_rows([grad_x], sizes), [grad_x.shape], sizes)
+    gain = jnp.pad(norm_gain[None, :], ((0, 7), (0, 0)))
+    grad_inputs, gain_sum = input_call(dz, gx, w_z, w_x, inputs, cotangent, gain, rows)
+    sums = sum_small(
         (
-            grad_norm_gain,
+            gain_sum[0],
             taps_sum[:4],
             taps_sum[4],
             heads_sum[0, :HEADS],
@@ -675,8 +888,11 @@
             gate_sums[1].reshape(HEADS, HEADDIM).sum(axis=1),
             gate_sums[0],
         ),
-        ("dp", "seq"),
-    )
+        sizes,
+    )
+
+
+    rows_in = jnp.concatenate([rows_z, rows_x[:, : width + HEADS]], axis=1)
     return (mixed, grad_inputs, rows_in, rows_out, *sums)
 
 
@@ -695,7 +911,7 @@
         P("dp", "seq", None),
     )
     return jax.shard_map(
-        functools.partial(body, mesh.shape["seq"]),
+        functools.partial(body, dict(mesh.shape)),
         mesh=mesh,
         in_specs=placed,
         out_specs=(

time: 723 us -> 493 us (0.68)
  waiting for transfers between devices: 238 us -> 78.3 us
  blocking collectives: 72.8 us -> 0 us
  matrix products: 72.1 us -> 17.2 us
  Pallas kernels: 185 us -> 239 us
  starting transfers between devices: 28.2 us -> 57 us
  other arithmetic: 64.8 us -> 38.9 us
    reduce_scatter x2 -> x0, waiting for transfers between devices: 158 us -> none  [the longest x1 158 us: body(): lax.psum_scatter(grad_in_full, 'seq', scatter_dimension=0, tiled=True)]
    all_gather x2 -> x1, waiting for transfers between devices: 73.4 us -> 2.36 us  [gather_later(): got = lax.all_gather(jnp.concatenate(halves, axis=0), 'seq', axis=0)]
    dot_general x11 -> x4, matrix products: 72.1 us -> 17.2 us  [project(): return jnp.dot(left, matrix, preferred_element_type=F32).astype(BF16)]
    pallas_call x0 -> x3, Pallas kernels: none -> 53.9 us  [the longest x1 19.4 us: input_call(): pl.pallas_call(input_kernel, grid=(seqs, length // rows), in_specs=[pl.Bl...]
    all_to_all x2 -> x6, waiting for transfers between devices: 0.01 us -> 41.6 us  [the longest x2 33.2 us: to_all(): return lax.all_to_all(copies, axes, split_axis=0, concat_axis=0, tiled=True)]
    psum x1 -> x0, blocking collectives: 41.4 us -> none  [body(): lax.psum((grad_norm_gain, taps_sum[:4], taps_sum[4], heads_sum[0, :HEADS]...]
    all_gather x1 -> x0, blocking collectives: 31.4 us -> none  [carry_over(): decay = jnp.exp(lax.all_gather(totals, 'seq', axis=0))]
    ppermute x0 -> x14, waiting for transfers between devices: none -> 21.9 us  [the longest x5 12.6 us: sum_small(): lax.ppermute(flat, axis, [(i, i ^ step) for i in range(sizes[axis])])]
  transfers between devices with their start and end apart: 11 -> 25, of which waited for: 5 -> 13; matrix products, arithmetic and copies ran while one was open for 23% -> 14% of each run, Pallas kernels for 20% -> 37%
where the time goes in v2:
time: 493 us; the launch traced here: 485 us
  Pallas kernels  239 us (48%)
  waiting for transfers between devices  78.3 us (16%)
  starting transfers between devices  57 us (12%)
  local copies, waits for them, and re-layouts  39.4 us (8%)
  other arithmetic  38.9 us (8%)
  matrix products  17.2 us (3%)
  between operations  15.1 us (3%)
    pallas_call x1, Pallas kernels, back_call(): pl.pallas_call(back_kernel, grid=(seqs, chunks), in_specs=[pl.BlockSpec((...  58.7 us
    pallas_call x1, Pallas kernels, finish_call(): pl.pallas_call(finish_kernel, grid=(seqs, length // rows), in_specs=[wide...  43.9 us
    pallas_call x1, Pallas kernels, gate_call(): pl.pallas_call(gate_kernel, grid=(seqs, length // rows), in_specs=[pl.Blo...  41.2 us
    pallas_call x1, Pallas kernels, scan_call(): pl.pallas_call(scan_kernel, grid=(seqs, chunks), in_specs=[pl.BlockSpec((...  40.9 us
    all_to_all x2, waiting for transfers between devices, to_all(): return lax.all_to_all(copies, axes, split_axis=0, concat_axis=0, tiled=True)  33.2 us
    pallas_call x1, Pallas kernels, input_call(): pl.pallas_call(input_kernel, grid=(seqs, length // rows), in_specs=[pl.Bl...  19.4 us
    pallas_call x1, Pallas kernels, taps_back_call(): pl.pallas_call(taps_back_kernel, grid=(seqs, length // rows), in_specs=[p...  18.1 us
    dot_general x4, matrix products, project(): return jnp.dot(left, matrix, preferred_element_type=F32).astype(BF16)  17.2 us
  transfers between devices with their start and end apart: 25, of which 13 were waited for; matrix products, arithmetic and copies ran while one was open for 14% of the time, Pallas kernels for 37%

profile of v2, /device:TPU:0, one launch (start us, length us, event | category | flops | bytes accessed | tf_op | source)
XLA Modules:
  0.0 484.6 jit_solution(13917058301701522322)
XLA Ops:
  9.5 7.4 %all-to-all-start = ((bf16[8,48,1920]{2,1,0:T(8,128)(2,1)}), bf16[8,48,1920]{2,1,0:T(8,128)(2,1)}, u32[]{:S(2)}, u32[]{:S(2)}) async-start(bf16[8,48,1920]{2,1,0:T(8,128)(2,1)} %broadcast_in_dim.20), calls=%async_computation | async-start | bytes 2949120 | tf_op jit(solution)/shard_map/all_to_all | solution.py:698
  17.0 3.9 collective-permute-start.1
  28.2 33.2 %all-to-all-done = bf16[8,48,1920]{2,1,0:T(8,128)(2,1)} async-done(((bf16[8,48,1920]{2,1,0:T(8,128)(2,1)}), bf16[8,48,1920]{2,1,0:T(8,128)(2,1)}, u32[]{:S(2)}, u32[]{:S(2)}) %all-to-all-start) | async-done | bytes 1474592 | tf_op jit(solution)/shard_map/all_to_all | solution.py:698
  72.6 3.7 all-to-all-start.1
  78.2 7.9 %fusion.xbc_ref.prev_ref = bf16[1,2048,1792]{2,1,0:T(8,128)(2,1)} fusion(bf16[1,2048,768]{2,1,0:T(8,128)(2,1)S(1)} %copy-done.5, bf16[768,1920]{1,0:T(8,128)(2,1)S(1)} %bitcast.111), kind=kOutput, calls=%fused_computation.4 | convolution fusion | flops 5640814592 | bytes 13238272 | tf_op jit(solution)/shard_map/dot_general | solution.py:843
  88.5 40.9 %scan_forward.1 = (bf16[1,2048,1792]{2,1,0:T(8,128)(2,1)}, f32[1,2048,1536]{2,1,0:T(8,128)}, f32[1,2048,128]{2,1,0:T(8,128)}, f32[1,2048,128]{2,1,0:T(8,128)}, f...) custom-call(bf16[1,2048,1792]{2,1,0:T(8,128)(2,1)} %fusion.xbc_ref.prev_ref, ...), custom_call_target="tpu_custom_call" | custom-call | flops 40960000000 | bytes 122880000 | tf_op jit(solution)/shard_map/scan_forward/pallas_call | solution.py:169
  131.5 3.8 all-to-all-start.2
  141.9 6.9 %fusion.1.z_ref = bf16[1,2048,1536]{2,1,0:T(8,128)(2,1)} fusion(bf16[768,1536]{1,0:T(8,128)(2,1)S(1)} %bitcast.121, bf16[1,2048,768]{2,1,0:T(8,128)(2,1)S(1)} %copy-done.6), kind=kOutput, calls=%fused_computation.5 | convolution fusion | flops 4834983936 | bytes 11796480 | tf_op jit(solution)/shard_map/dot_general | solution.py:843
  153.3 6.0 %all-to-all-start.3 = ((bf16[1,8,16,1536]{3,2,0,1:T(8,128)(2,1)}), bf16[1,8,16,1536]{3,2,0,1:T(8,128)(2,1)S(1)}, u32[]{:S(2)}, u32[]{:S(2)}) async-start(bf16[1,8,16,1536]{3,2,0,1:T(8,128)(2,1)} %fusion.31), calls=%async_computation.3 | async-start | bytes 786432 | tf_op jit(solution)/shard_map/all_to_all | solution.py:804
  163.2 7.9 %all-to-all-done.3 = bf16[1,8,16,1536]{3,2,0,1:T(8,128)(2,1)S(1)} async-done(((bf16[1,8,16,1536]{3,2,0,1:T(8,128)(2,1)}), bf16[1,8,16,1536]{3,2,0,1:T(8,128)(2,1)S(1)}, u32[]{:S(2)}, u32[]{:S(2)}) %all-to-all-start.3) | async-done | bytes 393248 | tf_op jit(solution)/shard_map/all_to_all | solution.py:804
  171.9 41.2 %gate_and_output.1 = (bf16[1,2048,768]{2,1,0:T(8,128)(2,1)}, bf16[1,2048,1536]{2,1,0:T(8,128)(2,1)}, bf16[1,2048,1536]{2,1,0:T(8,128)(2,1)}, bf16[1,2048,1536]{2...) custom-call(f32[1,2048,1536]{2,1,0:T(8,128)} %get-tuple-element.48.y, ...), custom_call_target="tpu_custom_call" | custom-call | flops 45056000000 | bytes 135168000 | tf_op jit(solution)/shard_map/gate_and_output/pallas_call | solution.py:269
  215.1 3.6 all-to-all-start.4
  218.7 16.5 %weight_gradients.1 = (f32[1536,768]{1,0:T(8,128)}, f32[768,1536]{1,0:T(8,128)}) custom-call(bf16[1,2048,1536]{2,1,0:T(8,128)(2,1)} %get-tuple-element.65.norm_ref, bf16[1,2048,768]{2,1,0:T(8,128)(2,1)} %c_ref.5, bf16[1,2048,768]{2,1,0:T(8,128)(2,1)} %fusion.4.n_ref.normed_ref, bf16[1,2048,1536]{2,1,0:T(8,128)(2,1)} %get-tuple-element.57.dz_ref), custom_call_target="tpu_custom_call" | custom-call | flops 16384000000 | bytes 49152000 | tf_op jit(solution)/shard_map/weight_gradients/pallas_call | solution.py:326
  245.5 6.0 %all-to-all-start.5 = ((bf16[1,8,16,1536]{3,2,0,1:T(8,128)(2,1)}), bf16[1,8,16,1536]{3,2,0,1:T(8,128)(2,1)S(1)}, u32[]{:S(2)}, u32[]{:S(2)}) async-start(bf16[1,8,16,1536]{3,2,0,1:T(8,128)(2,1)} %constant_dynamic-update-slice_fusion.1), calls=%async_computation.5 | async-start | bytes 786432 | tf_op jit(solution)/shard_map/all_to_all | solution.py:804
  251.5 58.7 %scan_backward.1 = (f32[1,2048,1792]{2,1,0:T(8,128)}, f32[1,2048,128]{2,1,0:T(8,128)}, f32[1,2048,128]{2,1,0:T(8,128)}) custom-call(bf16[1,2048,1792]{2,1,0:T(8,128)(2,1)} %get-tuple-element.49.act_ref, bf16[1,2048,1536]{2,1,0:T(8,128)(2,1)} %get-tuple-element.58.dy_ref, f32[1,2048,128]{2,1,0:T(8,128)} %get-tuple-element.59.dt_ref, ...), custom_call_target="tpu_custom_call" | custom-call | flops 59392000000 | bytes 178176000 | tf_op jit(solution)/shard_map/scan_backward/pallas_call | solution.py:443
  318.9 6.1 %all-to-all-start.6 = ((bf16[8,96,1536]{2,1,0:T(8,128)(2,1)}), bf16[8,96,1536]{2,1,0:T(8,128)(2,1)S(1)}, u32[]{:S(2)}, u32[]{:S(2)}) async-start(bf16[8,96,1536]{2,1,0:T(8,128)(2,1)} %pad_maximum_fusion), calls=%async_computation.6 | async-start | bytes 4718592 | tf_op jit(solution)/shard_map/all_to_all | solution.py:748
  326.2 43.9 %conv_backward.1 = (f32[1,2048,1792]{2,1,0:T(8,128)}, bf16[1,2048,128]{2,1,0:T(8,128)(2,1)}, f32[8,1792]{1,0:T(8,128)}, f32[8,128]{1,0:T(8,128)}) custom-call(f32[1,2048,1792]{2,1,0:T(8,128)} %get-tuple-element.63.g_ref, bf16[1,2048,1792]{2,1,0:T(8,128)(2,1)} %get-tuple-element.49.act_ref, bf16[1,2048,1792]{2,1,0:T(8,128)(2,1)} %fusion.xbc_ref.prev_ref, ...), custom_call_target="tpu_custom_call" | custom-call | flops 43008000000 | bytes 129024000 | tf_op jit(solution)/shard_map/conv_backward/pallas_call | solution.py:550
  370.1 8.4 %all-to-all-done.6 = bf16[8,96,1536]{2,1,0:T(8,128)(2,1)S(1)} async-done(((bf16[8,96,1536]{2,1,0:T(8,128)(2,1)}), bf16[8,96,1536]{2,1,0:T(8,128)(2,1)S(1)}, u32[]{:S(2)}, u32[]{:S(2)}) %all-to-all-start.6) | async-done | bytes 2359328 | tf_op jit(solution)/shard_map/all_to_all | solution.py:748
  380.8 4.5 collective-permute-done.5.after_ref
  386.0 18.1 %taps_backward.1 = (bf16[1,2048,1920]{2,1,0:T(8,128)(2,1)}, f32[768,1920]{1,0:T(8,128)}) custom-call(f32[1,2048,1792]{2,1,0:T(8,128)} %get-tuple-element.75.g_ref.next_ref, f32[1,2048,1792]{2,1,0:T(8,128)} %get-tuple-element.75.g_ref.next_ref, f32[1,8,1792]{2,1,0:T(8,128)} %copy-done.21, bf16[1,2048,128]{2,1,0:T(8,128)(2,1)} %get-tuple-element.76.gdt_ref, ...), custom_call_target="tpu_custom_call" | custom-call | flops 18432000000 | bytes 55296000 | tf_op jit(solution)/shard_map/taps_backward/pallas_call | solution.py:626
  410.8 3.7 fusion.9
  414.5 4.3 all-to-all-start.7
  418.8 19.4 %input_gradient.1 = (f32[1,2048,768]{2,1,0:T(8,128)}, f32[8,768]{1,0:T(8,128)}) custom-call(bf16[1,2048,1536]{2,1,0:T(8,128)(2,1)} %get-tuple-element.57.dz_ref, bf16[1,2048,1920]{2,1,0:T(8,128)(2,1)} %get-tuple-element.77.gx_ref, bf16[768,1536]{1,0:T(8,128)(2,1)} %bitcast.122, bf16[768,1920]{1,0:T(8,128)(2,1)} %bitcast.112, bf16[1,2048,768]{2,1,0:T(8,128)(2,1)} %u_ref.3, ...), custom_call_target="tpu_custom_call" | custom-call | flops 18432000000 | bytes 55296000 | tf_op jit(solution)/shard_map/input_gradient/pallas_call | solution.py:673
  466.8 7.5 %collective-permute-done.9 = f32[48,1920]{1,0:T(8,128)S(1)} collective-permute-done((f32[48,1920]{1,0:T(8,128)S(1)}, f32[48,1920]{1,0:T(8,128)S(1)}, u32[]{:S(2)}, u32[]{:S(2)}) %collective-permute-start.9) | collective-permute-done | bytes 368672 | tf_op jit(solution)/shard_map/ppermute | solution.py:757
  (196 shorter events, 106.0 us)
Async XLA Ops:
  9.5 51.9 %all-to-all-start = ((bf16[8,48,1920]{2,1,0:T(8,128)(2,1)}), bf16[8,48,1920]{2,1,0:T(8,128)(2,1)}, u32[]{:S(2)}, u32[]{:S(2)}) async-start(bf16[8,48,1920]{2,1,0:T(8,128)(2,1)} %broadcast_in_dim.20), calls=%async_computation | async-start | bytes 2949120 | tf_op jit(solution)/shard_map/all_to_all | solution.py:698
  16.9 71.5 %all-gather.3.cloned.1.call-start = ((), (), s32[]{:S(2)}) async-start(), calls=%async_computation.8 | async-start | bytes 2654208 | tf_op jit(solution)/shard_map/all_gather | solution.py:724
  17.0 49.3 %collective-permute-start.1 = (bf16[1,16,768]{2,1,0:T(8,128)(2,1)S(1)}, bf16[1,16,768]{2,1,0:T(8,128)(2,1)S(1)}, u32[]{:S(2)}, u32[]{:S(2)}) collective-permute-start(bf16[1,16,768]{2,1,0:T(8,128)(2,1)S(1)} %slice.174), channel_id=1, source_target_pairs={{0,1},{1,2},{2,3},{3,4},{4,5},{5,6},{6,7},{8,9},{9,10},{10,11},{11... | collective-permute-start | bytes 73736 | tf_op jit(solution)/shard_map/ppermute | solution.py:787
  61.4 5.0 %collective-permute-start = (bf16[8,48,1920]{2,1,0:T(8,128)(2,1)}, bf16[8,48,1920]{2,1,0:T(8,128)(2,1)}, u32[]{:S(2)}, u32[]{:S(2)}) collective-permute-start(bf16[8,48,1920]{2,1,0:T(8,128)(2,1)} %all-to-all-done), channel_id=1, source_target_pairs={{0,8},{8,0},{16,24},{24,16},{1,9},{9,1},{17,25},{25,17},{2,10},{10... | collective-permute-start | bytes 4423688 | tf_op jit(solution)/shard_map/ppermute | solution.py:702
  72.6 56.8 %all-to-all-start.1 = ((f32[8,1,128]{2,1,0:T(1,128)}), f32[8,1,128]{2,1,0:T(1,128)S(1)}, u32[]{:S(2)}, u32[]{:S(2)}) async-start(f32[8,1,128]{2,1,0:T(1,128)} %broadcast_in_dim.22), calls=%async_computation.1 | async-start | bytes 8192 | tf_op jit(solution)/shard_map/all_to_all | solution.py:698
  88.5 48.9 %collective-permute-start.2 = (bf16[8,96,1536]{2,1,0:T(8,128)(2,1)}, bf16[8,96,1536]{2,1,0:T(8,128)(2,1)}, u32[]{:S(2)}, u32[]{:S(2)}) collective-permute-start(bf16[8,96,1536]{2,1,0:T(8,128)(2,1)} %bitcast.123), channel_id=1, source_target_pairs={{0,8},{8,0},{16,24},{24,16},{1,9},{9,1},{17,25},{25,17},{2,10},{10... | collective-permute-start | bytes 7077896 | tf_op jit(solution)/shard_map/ppermute | solution.py:702
  131.5 17.2 %all-to-all-start.2 = ((bf16[1,8,16,1536]{3,2,0,1:T(8,128)(2,1)}), bf16[1,8,16,1536]{3,2,0,1:T(8,128)(2,1)S(1)}, u32[]{:S(2)}, u32[]{:S(2)}) async-start(bf16[1,8,16,1536]{3,2,0,1:T(8,128)(2,1)} %bitcast.14), calls=%async_computation.2 | async-start | bytes 786432 | tf_op jit(solution)/shard_map/all_to_all | solution.py:794
  153.3 17.8 %all-to-all-start.3 = ((bf16[1,8,16,1536]{3,2,0,1:T(8,128)(2,1)}), bf16[1,8,16,1536]{3,2,0,1:T(8,128)(2,1)S(1)}, u32[]{:S(2)}, u32[]{:S(2)}) async-start(bf16[1,8,16,1536]{3,2,0,1:T(8,128)(2,1)} %fusion.31), calls=%async_computation.3 | async-start | bytes 786432 | tf_op jit(solution)/shard_map/all_to_all | solution.py:804
  215.1 20.1 %all-to-all-start.4 = ((bf16[1,8,16,1536]{3,2,0,1:T(8,128)(2,1)}), bf16[1,8,16,1536]{3,2,0,1:T(8,128)(2,1)S(1)}, u32[]{:S(2)}, u32[]{:S(2)}) async-start(bf16[1,8,16,1536]{3,2,0,1:T(8,128)(2,1)} %bitcast.24), calls=%async_computation.4 | async-start | bytes 786432 | tf_op jit(solution)/shard_map/all_to_all | solution.py:794
  237.0 75.1 %collective-permute-start.3 = (bf16[8,96,768]{2,1,0:T(8,128)(2,1)S(1)}, bf16[8,96,768]{2,1,0:T(8,128)(2,1)}, u32[]{:S(2)}, u32[]{:S(2)}) collective-permute-start(bf16[8,96,768]{2,1,0:T(8,128)(2,1)S(1)} %fusion.17), channel_id=1, source_target_pairs={{0,8},{8,0},{16,24},{24,16},{1,9},{9,1},{17,25},{25,17},{2,10},{10... | collective-permute-start | bytes 3538952 | tf_op jit(solution)/shard_map/ppermute | solution.py:702
  239.9 75.0 %collective-permute-start.4 = (bf16[8,48,1536]{2,1,0:T(8,128)(2,1)}, bf16[8,48,1536]{2,1,0:T(8,128)(2,1)}, u32[]{:S(2)}, u32[]{:S(2)}) collective-permute-start(bf16[8,48,1536]{2,1,0:T(8,128)(2,1)} %fusion.18), channel_id=1, source_target_pairs={{0,8},{8,0},{16,24},{24,16},{1,9},{9,1},{17,25},{25,17},{2,10},{10... | collective-permute-start | bytes 3538952 | tf_op jit(solution)/shard_map/ppermute | solution.py:702
  245.5 66.2 %all-to-all-start.5 = ((bf16[1,8,16,1536]{3,2,0,1:T(8,128)(2,1)}), bf16[1,8,16,1536]{3,2,0,1:T(8,128)(2,1)S(1)}, u32[]{:S(2)}, u32[]{:S(2)}) async-start(bf16[1,8,16,1536]{3,2,0,1:T(8,128)(2,1)} %constant_dynamic-update-slice_fusion.1), calls=%async_computation.5 | async-start | bytes 786432 | tf_op jit(solution)/shard_map/all_to_all | solution.py:804
  318.9 59.6 %all-to-all-start.6 = ((bf16[8,96,1536]{2,1,0:T(8,128)(2,1)}), bf16[8,96,1536]{2,1,0:T(8,128)(2,1)S(1)}, u32[]{:S(2)}, u32[]{:S(2)}) async-start(bf16[8,96,1536]{2,1,0:T(8,128)(2,1)} %pad_maximum_fusion), calls=%async_computation.6 | async-start | bytes 4718592 | tf_op jit(solution)/shard_map/all_to_all | solution.py:748
  379.3 6.1 %collective-permute-start.5 = (f32[1,8,1792]{2,1,0:T(8,128)S(1)}, f32[1,8,1792]{2,1,0:T(8,128)S(1)}, u32[]{:S(2)}, u32[]{:S(2)}) collective-permute-start(f32[1,8,1792]{2,1,0:T(8,128)S(1)} %slice.205), channel_id=1, source_target_pairs={{1,0},{2,1},{3,2},{4,3},{5,4},{6,5},{7,6},{9,8},{10,9},{11,10},{12... | collective-permute-start | bytes 172040 | tf_op jit(solution)/shard_map/ppermute | solution.py:787
  407.2 3.6 collective-permute-start.8
  414.5 47.2 %all-to-all-start.7 = ((bf16[8,48,1920]{2,1,0:T(8,128)(2,1)}), bf16[8,48,1920]{2,1,0:T(8,128)(2,1)}, u32[]{:S(2)}, u32[]{:S(2)}) async-start(bf16[8,48,1920]{2,1,0:T(8,128)(2,1)} %fusion.9), calls=%async_computation.7 | async-start | bytes 2949120 | tf_op jit(solution)/shard_map/all_to_all | solution.py:748
  440.3 4.2 collective-permute-start.12
  442.2 18.8 %collective-permute-start.6 = (f32[96,1536]{1,0:T(8,128)S(1)}, f32[96,1536]{1,0:T(8,128)S(1)}, u32[]{:S(2)}, u32[]{:S(2)}) collective-permute-start(f32[96,1536]{1,0:T(8,128)S(1)} %convert_reduce_fusion), channel_id=1, source_target_pairs={{0,16},{8,24},{16,0},{24,8},{1,17},{9,25},{17,1},{25,9},{2,18},{10... | collective-permute-start | bytes 1769480 | tf_op jit(solution)/shard_map/ppermute | solution.py:757
  444.5 5.8 %collective-permute-start.13 = (f32[96,128]{1,0:T(8,128)S(1)}, f32[96,128]{1,0:T(8,128)S(1)}, u32[]{:S(2)}, u32[]{:S(2)}) collective-permute-start(f32[96,128]{1,0:T(8,128)S(1)} %fusion.49), channel_id=1, source_target_pairs={{0,1},{1,0},{2,3},{3,2},{4,5},{5,4},{6,7},{7,6},{8,9},{9,8},{10,11... | collective-permute-start | bytes 147464 | tf_op jit(solution)/shard_map/ppermute | solution.py:775
  450.3 5.0 %collective-permute-start.14 = (f32[96,128]{1,0:T(8,128)S(1)}, f32[96,128]{1,0:T(8,128)S(1)}, u32[]{:S(2)}, u32[]{:S(2)}) collective-permute-start(f32[96,128]{1,0:T(8,128)S(1)} %add.328), channel_id=1, source_target_pairs={{0,2},{1,3},{2,0},{3,1},{4,6},{5,7},{6,4},{7,5},{8,10},{9,11},{10,... | collective-permute-start | bytes 147464 | tf_op jit(solution)/shard_map/ppermute | solution.py:775
  455.2 5.1 %collective-permute-start.15 = (f32[96,128]{1,0:T(8,128)S(1)}, f32[96,128]{1,0:T(8,128)S(1)}, u32[]{:S(2)}, u32[]{:S(2)}) collective-permute-start(f32[96,128]{1,0:T(8,128)S(1)} %add.329), channel_id=1, source_target_pairs={{0,4},{1,5},{2,6},{3,7},{4,0},{5,1},{6,2},{7,3},{8,12},{9,13},{10,... | collective-permute-start | bytes 147464 | tf_op jit(solution)/shard_map/ppermute | solution.py:775
  461.0 5.7 %collective-permute-start.7 = (f32[96,1536]{1,0:T(8,128)S(1)}, f32[96,1536]{1,0:T(8,128)S(1)}, u32[]{:S(2)}, u32[]{:S(2)}) collective-permute-start(f32[96,1536]{1,0:T(8,128)S(1)} %add.323), channel_id=1, source_target_pairs={{0,8},{8,0},{16,24},{24,16},{1,9},{9,1},{17,25},{25,17},{2,10},{10... | collective-permute-start | bytes 1769480 | tf_op jit(solution)/shard_map/ppermute | solution.py:702
  463.3 11.1 %collective-permute-start.9 = (f32[48,1920]{1,0:T(8,128)S(1)}, f32[48,1920]{1,0:T(8,128)S(1)}, u32[]{:S(2)}, u32[]{:S(2)}) collective-permute-start(f32[48,1920]{1,0:T(8,128)S(1)} %convert_reduce_fusion.1), channel_id=1, source_target_pairs={{0,16},{8,24},{16,0},{24,8},{1,17},{9,25},{17,1},{25,9},{2,18},{10... | collective-permute-start | bytes 1105928 | tf_op jit(solution)/shard_map/ppermute | solution.py:757
  474.4 1.8 collective-permute-start.10
  (24 other events, 239.6 us)
Sparse Core Ops, SparseCore 0:
  26.0 62.3 all-gather.2
